TPU v7x, 512 devices: a whole 4x8x8 slice. The times are simulated.
512 devices in a mesh: row: 16 (over z, core), col: 32 (over x, y).
Axes of the slice: x: 4, y: 8, z: 8, core: 2. Of those that a mesh axis runs over, the one named last changes fastest.
Arguments:
- hamiltonian: float32 [12288, 12288], P('row', 'col'), may hold values from -5 to 5, as said below
- factor_rows: float32 [128, 12288], P(None, 'col'), may hold values from -0.5 to 3, as said below
Outputs:
- state: float32 [12288, 12288], P('row', 'col')
Inputs may be any that keep to these rules, and one draw needn't show every extreme that they name: In global order hamiltonian is symmetric. In global column order, row k of factor_rows is zero at columns before k and lies in 1.5 to 3 at column k.
All inputs are finite; a program needn't handle non-finite values.
Results may differ from a plain program's by a relative error of at most 0.0001.
Values sent between devices are 32-bit elements; how exact they have to be, the bound alone decides.
No kernel may reach another device: no remote copies, remote signals or barrier semaphores. Data moves between devices by JAX's collectives and lax.ppermute only.
A program may use at most 64 MiB of HBM per device.

v0:
```python
import jax
import jax.numpy as jnp
from jax import lax
from jax.sharding import PartitionSpec as P

BLOCK = 64


def spread(block, axis, holder):
    block = jnp.where(lax.axis_index(axis) == holder, block, jnp.zeros_like(block))
    return lax.psum(block, axis)


def matmul(left_side, right_side):
    return jnp.dot(
        left_side, right_side, precision=lax.Precision.HIGHEST, preferred_element_type=jnp.float32
    )


def inner(left_side, right_side):
    return lax.dot_general(
        left_side,
        right_side,
        (((0,), (0,)), ((), ())),
        precision=lax.Precision.HIGHEST,
        preferred_element_type=jnp.float32,
    )


def upper_inverse(factor):
    width = factor.shape[0]
    diag_entries = jnp.diagonal(factor)
    power = -(jnp.triu(factor, 1) / diag_entries[:, None])
    total = jnp.eye(width, dtype=factor.dtype) + power
    for _ in range((width - 1).bit_length() - 1):
        power = matmul(power, power)
        total = total + matmul(total, power)
    return total / diag_entries[None, :]


def left_solve(factor, right_side):
    return inner(upper_inverse(factor), right_side)


def right_solve(factor, left_side):
    return matmul(left_side, upper_inverse(factor))


def congruence(factor, matrix):
    inverse = upper_inverse(factor)
    return matmul(inner(inverse, matrix), inverse)


def panel_rest(diag_factor, result, panel_rows, factor_cols):
    solved = left_solve(diag_factor, panel_rows)
    shifted = matmul(result, factor_cols)
    halfway = solved - 0.5 * shifted
    pending = halfway - 0.5 * shifted
    return (halfway, pending)


def per_device(hamiltonian, factor_rows):
    block_width = BLOCK
    grid_rows = lax.axis_size("row")
    grid_cols = lax.axis_size("col")
    row_index = lax.axis_index("row")
    col_index = lax.axis_index("col")
    local_rows, local_cols = hamiltonian.shape
    col_blocks = local_cols // block_width
    folding = grid_cols // grid_rows
    col_ids = jnp.repeat(
        jnp.arange(col_blocks, dtype=jnp.int32) * grid_cols + col_index, block_width
    )
    row_ids = jnp.repeat(
        jnp.arange(local_rows // block_width, dtype=jnp.int32) * grid_rows + row_index, block_width
    )

    def reorder(pieces):
        stacked = jnp.stack(pieces)
        count = stacked.shape[0]
        height = stacked.shape[1]
        arranged = stacked.reshape(count, height, col_blocks, block_width).transpose(1, 2, 0, 3)
        return arranged.reshape(height, col_blocks * count * block_width)

    def down(payload, source):
        return spread(payload, "row", source)

    def mirror(payload):
        mirrored = reorder(
            [spread(payload, "col", row_index + section * grid_rows) for section in range(folding)]
        )
        return mirrored

    lead_factor, lead_block = (
        spread(factor_rows[:block_width, :block_width], "col", 0),
        spread(hamiltonian[:block_width, :block_width], "col", 0),
    )
    next_factor = spread(factor_rows[:, :block_width], "col", 1)
    factor_mirror = reorder(
        [spread(factor_rows, "col", row_index + section * grid_rows) for section in range(folding)]
    )
    next_diag = next_factor[block_width:]
    lead_result = congruence(lead_factor, lead_block)
    lead_half, lead_pending = panel_rest(
        lead_factor, lead_result, hamiltonian[:block_width], factor_rows[:block_width]
    )
    past_first = col_ids[None, :] >= 1
    upper_cols = jnp.where(past_first, factor_rows[:block_width], 0.0)
    lead_half = jnp.where(past_first, lead_half, 0.0)
    lead_cols = down(lead_half, 0)
    lead_rows = mirror(lead_cols)
    upper_rows = jnp.where(row_ids[None, :] >= 1, factor_mirror[:block_width], 0.0)
    updated = hamiltonian - (inner(upper_rows, lead_cols) + inner(lead_rows, upper_cols))
    pivot_rows = updated[:block_width]
    own_couple = right_solve(next_diag, lead_pending[:, :block_width])
    own_next = congruence(next_diag, pivot_rows[:, :block_width])
    received = spread(jnp.where(row_index == 0, own_couple, own_next), "col", 1)
    lower_source = factor_rows[block_width:]
    next_half, next_pending = panel_rest(next_diag, received, pivot_rows, lower_source)
    lead_remain = lead_pending - matmul(received, lower_source)
    past_second = col_ids[None, :] >= 2
    next_half = jnp.where(past_second, next_half, 0.0)
    lower_cols = jnp.where(past_second, lower_source, 0.0)
    next_cols = down(next_half, 1)
    next_rows = mirror(next_cols)
    lower_rows = jnp.where(row_ids[None, :] >= 2, factor_mirror[block_width:], 0.0)
    trailing = updated - (inner(lower_rows, next_cols) + inner(next_rows, lower_cols))
    inside_mask = (row_ids[:, None] >= 2) & (col_ids[None, :] >= 2)
    merged = jnp.where(inside_mask, trailing, hamiltonian)
    first_col = col_ids[None, :] == 0
    second_col = col_ids[None, :] == 1
    lead_top = jnp.where(
        first_col,
        jnp.tile(lead_result, (1, col_blocks)),
        jnp.where(second_col, jnp.tile(received, (1, col_blocks)), lead_remain),
    )
    next_top = jnp.where(
        first_col,
        hamiltonian[:block_width],
        jnp.where(second_col, jnp.tile(received, (1, col_blocks)), next_pending),
    )
    top_rows = jnp.where(
        row_index == 0, lead_top, jnp.where(row_index == 1, next_top, merged[:block_width])
    )
    return jnp.concatenate([top_rows, merged[block_width:]], 0)


def solution(mesh):
    placed = (P("row", "col"), P(None, "col"))
    return jax.shard_map(
        per_device, mesh=mesh, in_specs=placed, out_specs=P("row", "col"), check_vma=False
    )
```

profile of v0, /device:TPU:1, one launch (start us, length us, event | category | flops | bytes accessed | tf_op | source)
XLA Modules:
  0.0 874.4 jit_solution(5683695280117807636)
XLA Ops:
  6.5 1.5 slice_select_fusion.1
  8.0 1.4 slice_select_fusion.2
  9.5 1.1 copy.3
  11.1 0.8 broadcast_select_fusion.1
  11.9 153.2 %all-reduce.13.cloned.1.call-done = (f32[64,64]{1,0:T(8,128)}, f32[64,64]{1,0:T(8,128)}, f32[128,64]{1,0:T(8,128)}) async-done(((f32[64,64]{1,0:T(8,128)}, f32[64,64]{1,0:T(8,128)}, f32[128,64]{1,0:T(8,128)}), (f32[64,64]{1,0:T(8,128)}, f32[64,64]{1,0:T(8,128)}, f32[128,64]{1,0:T(8,128)})) %all-reduce.13.cloned.1.call-update) | async-done | bytes 65552 | tf_op jit(solution)/shard_map/psum | solution.py:11
  165.1 1.6 gather_fusion
  166.7 1.1 fusion.38
  167.8 1.0 convolution_add_fusion.11
  169.0 0.9 slice.72
  169.8 0.8 gather_fusion.1
  170.6 0.2 fusion.39
  170.9 0.2 convolution_add_fusion.6
  172.5 0.2 fusion.48
  172.9 0.2 convolution_multiply_fusion
  173.2 0.9 fusion.43
  175.0 112.2 %all-reduce.9.cloned.1.call-done = f32[64,384]{1,0:T(8,128)} async-done(((f32[64,384]{1,0:T(8,128)}), f32[64,384]{1,0:T(8,128)}) %all-reduce.9.cloned.1.call-update) | async-done | bytes 98320 | tf_op jit(solution)/shard_map/psum | solution.py:11
  287.2 0.9 broadcast_select_fusion.4
  288.1 0.8 stack.30
  288.9 0.8 stack.31
  290.3 156.7 %all-reduce.17.cloned.1.call-done = (f32[1,128,6,64]{1,3,2,0:T(8,128)}, f32[1,128,6,64]{1,3,2,0:T(8,128)}, f32[1,64,6,64]{3,2,1,0:T(8,128)}, f32[1,64,6,64]{3,2,1,0:T(8,128)}) async-done(((f32[1,128,6,64]{1,3,2,0:T(8,128)}, f32[1,128,6,64]{1,3,2,0:T(8,128)}, f32[1,64,6,64]{3,2,1,0:T(8,128)}, f32[1,64,6,64]{3,2,1,0:T(8,128)}), (f32[1,128,6,64]{1,3,2,0:T(8,128)}, f32[1,128,6,64]{1,3,2,0:T(8,128)}, ...) | async-done | bytes 589840 | tf_op jit(solution)/shard_map/psum | solution.py:11
  447.0 1.1 maximum_bitcast_fusion
  448.1 0.3 copy.6
  448.4 0.3 reshape.97
  448.8 0.2 fusion.42
  449.0 0.3 copy.5
  449.3 0.3 slice.59
  449.7 1.1 fusion.8
  450.9 1.2 fusion.2
  452.0 0.2 fusion.28
  452.5 112.9 %psum.92 = f32[64,64]{1,0:T(8,128)S(1)} all-reduce(f32[64,64]{1,0:T(8,128)S(1)} %fusion.5), channel_id=1, replica_groups=mesh['row'=16,'col'=32] {'col'}, use_global_device_ids=true, to_apply=%region_8.9 | all-reduce | flops 4096 | bytes 32768 | tf_op jit(solution)/shard_map/psum | solution.py:11
  565.3 0.2 fusion.19
  565.5 1.0 select_select_fusion
  567.1 0.7 tile.9
  567.9 0.3 copy.7
  568.1 1.0 slice.64
  569.2 0.7 tile.11
  569.9 132.4 %all-reduce.11.cloned.1.call-done = f32[64,384]{1,0:T(8,128)} async-done(((f32[64,384]{1,0:T(8,128)}), f32[64,384]{1,0:T(8,128)}) %all-reduce.11.cloned.1.call-update) | async-done | bytes 98320 | tf_op jit(solution)/shard_map/psum | solution.py:11
  702.3 0.9 broadcast_select_fusion.2
  703.2 0.8 stack.33
  704.0 0.8 stack.34
  704.8 2.1 fusion.6
  707.0 152.3 %all-reduce.15.cloned.1.call-done = (f32[1,64,6,64]{3,2,1,0:T(8,128)}, f32[1,64,6,64]{3,2,1,0:T(8,128)}) async-done(((f32[1,64,6,64]{3,2,1,0:T(8,128)}, f32[1,64,6,64]{3,2,1,0:T(8,128)}), (f32[1,64,6,64]{3,2,1,0:T(8,128)}, f32[1,64,6,64]{3,2,1,0:T(8,128)})) %all-reduce.15.cloned.1.call-update) | async-done | bytes 196624 | tf_op jit(solution)/shard_map/psum | solution.py:11
  859.2 1.1 maximum_bitcast_fusion.1
  860.3 1.1 copy.8
  861.4 2.0 reshape.98
  863.4 2.2 fusion.1
  865.8 0.8 copy-done.3
  866.8 1.1 pad_maximum_fusion
  (79 shorter events, 4.8 us)
Async XLA Ops:
  6.5 158.5 %all-reduce.13.cloned.1.call-start = ((), (), s32[]{:S(2)}) async-start(), calls=%async_computation.2 | async-start | bytes 262144 | tf_op jit(solution)/shard_map/psum | solution.py:11
  9.4 277.8 %all-reduce.9.cloned.1.call-start = ((), (), s32[]{:S(2)}) async-start(), calls=%async_computation | async-start | bytes 196608 | tf_op jit(solution)/shard_map/psum | solution.py:11
  165.1 5.6 copy-start.13
  166.7 5.8 copy-start.12
  166.7 6.2 copy-start.1
  168.8 4.3 copy-start
  174.1 116.0 %copy-start.4 = (f32[64,384]{1,0:T(8,128)}, f32[64,384]{1,0:T(8,128)S(1)}, u32[]{:S(2)}) copy-start(f32[64,384]{1,0:T(8,128)S(1)} %get-tuple-element.20) | copy-start | bytes 294916
  174.1 272.8 %all-reduce.17.cloned.1.call-start = ((), (), s32[]{:S(2)}) async-start(), calls=%async_computation.4 | async-start | bytes 1835008 | tf_op jit(solution)/shard_map/psum | solution.py:11
  289.7 412.6 %all-reduce.11.cloned.1.call-start = ((), (), s32[]{:S(2)}) async-start(), calls=%async_computation.1 | async-start | bytes 196608 | tf_op jit(solution)/shard_map/psum | solution.py:11
  447.0 1.8 copy-start.10
  447.0 1.8 copy-start.11
  448.8 0.9 copy-start.6
  565.5 1.5 copy-start.2
  566.6 292.7 %all-reduce.15.cloned.1.call-start = ((), (), s32[]{:S(2)}) async-start(), calls=%async_computation.3 | async-start | bytes 1048576 | tf_op jit(solution)/shard_map/psum | solution.py:11
  865.6 0.9 copy-start.3
  865.6 0.9 copy-start.5
  865.6 1.0 copy-start.7
  865.7 1.0 copy-start.8
  865.7 1.1 copy-start.9
Sparse Core Ops, SparseCore 0:
  11.1 153.9 all-reduce.12
  174.3 112.9 all-reduce.8
  291.0 155.9 all-reduce.16
  566.7 135.5 all-reduce.10
  706.0 153.2 all-reduce.14
where the time goes:
time: 878 us; the launch traced here: 874 us
  waiting for transfers between devices  707 us (81%)
  blocking collectives  113 us (13%)
  local copies, waits for them, and re-layouts  16.9 us (2%)
  matrix products  15.1 us (2%)
  between operations  13.6 us (2%)
  other arithmetic  8.92 us (1%)
    psum x5, waiting for transfers between devices, spread(): return lax.psum(block, axis)  707 us
    psum x1, blocking collectives, spread(): return lax.psum(block, axis)  113 us
  transfers between devices with their start and end apart: 5, of which 5 were waited for; matrix products, arithmetic and copies ran while one was open for 1% of the time, Pallas kernels for 0%

commit v1 on v0

v1 whole, which is shorter than its diff:
```python
import jax
import jax.numpy as jnp
from jax import lax
from jax.experimental import pallas as pl
from jax.experimental.pallas import tpu as pltpu
from jax.sharding import PartitionSpec as P

BLOCK = 64
WIDE = 2 * BLOCK
EXACT = lax.Precision.HIGHEST


def dot(left, right):
    return jnp.dot(left, right, precision=EXACT, preferred_element_type=jnp.float32)


def inner(left, right):
    return lax.dot_general(
        left, right, (((0,), (0,)), ((), ())), precision=EXACT, preferred_element_type=jnp.float32
    )


def wide_inverse(factor):
    row = lax.broadcasted_iota(jnp.int32, (WIDE, WIDE), 0)
    col = lax.broadcasted_iota(jnp.int32, (WIDE, WIDE), 1)
    on_diag = jnp.where(row == col, factor, 0.0)
    diag_col = jnp.sum(on_diag, axis=1, keepdims=True)
    diag_row = jnp.sum(on_diag, axis=0, keepdims=True)
    same = (row < BLOCK) == (col < BLOCK)
    power = jnp.where((row < col) & same, -factor / diag_col, 0.0)
    total = jnp.where(row == col, 1.0, power)
    for _ in range(5):
        power = dot(power, power)
        total = total + dot(total, power)
    total = total / diag_row
    couple = jnp.where((row < BLOCK) & (col >= BLOCK), factor, 0.0)
    return total - dot(total, dot(couple, total))


def body(
    place, h_ref, rj_ref, hj_ref, ra_ref, rb_ref, ha_ref, hb_ref, factor_ref, corner_ref, out_ref
):
    grid_row, grid_col = place[0], place[1]
    inverse = wide_inverse(factor_ref[...])
    result = dot(inner(inverse, corner_ref[...]), inverse)
    width = rj_ref.shape[1]
    weights = jnp.concatenate([inverse.T, -0.5 * result], axis=1)
    r_own, h_own = rj_ref[...], hj_ref[...]
    z_own = dot(weights, jnp.concatenate([h_own, r_own], axis=0))
    right = jnp.concatenate([z_own, r_own], axis=0)
    lane = lax.broadcasted_iota(jnp.int32, (BLOCK, width), 1)
    inside = (lane >= BLOCK) | (grid_col >= 2)
    parity = lax.rem(grid_col, 2)
    for order, (r_piece, h_piece) in enumerate(((ra_ref, ha_ref), (rb_ref, hb_ref))):
        r_rows = r_piece[...]
        z_rows = dot(weights, jnp.concatenate([h_piece[...], r_rows], axis=0))
        change = inner(jnp.concatenate([r_rows, z_rows], axis=0), right)
        section = parity if order == 0 else 1 - parity
        for m in range(width // BLOCK):
            rows = pl.ds(pl.multiple_of((2 * m + section) * BLOCK, BLOCK), BLOCK)
            part = change[m * BLOCK : (m + 1) * BLOCK]
            out_ref[rows, :] = h_ref[rows, :] - jnp.where(inside, part, 0.0)

    @pl.when(grid_row < 2)
    def _():
        pending = z_own - 0.5 * dot(result, r_own)
        old = h_ref[:BLOCK, :]
        first = grid_row == 0
        rest = jnp.where(first, pending[:BLOCK], pending[BLOCK:])
        lead = jnp.where(first, result[:BLOCK], result[BLOCK:])
        spread = jnp.concatenate([lead] * (width // WIDE), axis=1)
        turned = jnp.concatenate([lead[:, BLOCK:], lead[:, :BLOCK]] * (width // WIDE), axis=1)
        at_zero = jnp.where(first, spread, old)
        head = jnp.where(grid_col == 0, at_zero, turned)
        out_ref[:BLOCK, :] = jnp.where(inside, rest, head)


def finish(place, *operands):
    hamiltonian = operands[0]
    vmem = pl.BlockSpec(memory_space=pltpu.VMEM)
    return pl.pallas_call(
        body,
        out_shape=jax.ShapeDtypeStruct(hamiltonian.shape, jnp.float32),
        in_specs=[pl.BlockSpec(memory_space=pltpu.SMEM)] + [vmem] * len(operands),
        out_specs=vmem,
        compiler_params=pltpu.CompilerParams(vmem_limit_bytes=40 * 1024 * 1024),
        cost_estimate=pl.CostEstimate(flops=10**9, bytes_accessed=5 * 10**6, transcendentals=0),
    )(place, *operands)


def exchange(payload, axis):
    return lax.all_to_all(payload, axis, 0, 0)


def offer(payload, axis, count):
    return exchange(jnp.broadcast_to(payload[None], (count, *payload.shape)), axis)


def per_device(hamiltonian, factor_rows):
    grid_rows, grid_cols = lax.axis_size("row"), lax.axis_size("col")
    row_index, col_index = lax.axis_index("row"), lax.axis_index("col")
    width = hamiltonian.shape[1]
    slab = BLOCK // grid_rows

    def turn(payload):
        direct, crossed = [], []
        for r in range(grid_rows):
            for c in range(grid_cols):
                source = r * grid_cols + c
                row, section = c % grid_rows, c // grid_rows
                direct.append((source, row * grid_cols + 2 * r + section))
                crossed.append((source, row * grid_cols + 2 * r + 1 - section))
        axes = ("row", "col")
        return lax.ppermute(payload, axes, direct), lax.ppermute(payload, axes, crossed)

    ra, rb = turn(factor_rows)
    top = hamiltonian[:BLOCK].reshape(grid_rows, slab, width)
    mine = exchange(top, "row")[:2]
    panel = offer(mine, "row", grid_rows)
    panel = panel.transpose(1, 0, 2, 3).reshape(WIDE, width)
    lead = factor_rows[:, :BLOCK].reshape(2, grid_rows, slab, BLOCK)
    lead = lax.dynamic_index_in_dim(lead, row_index, 1, keepdims=False)
    pieces = offer(jnp.stack([lead, mine[:, :, :BLOCK]]), "col", grid_cols)[:2]
    pieces = offer(pieces, "row", grid_rows)
    pieces = pieces.transpose(2, 3, 0, 4, 1, 5).reshape(2, WIDE, WIDE)
    ha, hb = turn(panel)
    place = jnp.stack([row_index, col_index])
    return finish(
        place, hamiltonian, factor_rows, panel, ra, rb, ha, hb, pieces[0], pieces[1]
    )


def solution(mesh):
    placed = (P("row", "col"), P(None, "col"))
    return jax.shard_map(
        per_device, mesh=mesh, in_specs=placed, out_specs=P("row", "col"), check_vma=False
    )
```

time: 878 us -> 125 us (0.14)
  the two profiles are of different devices: /device:TPU:1 before, /device:TPU:201 now
where the time goes in v1:
time: 125 us; the launch traced here: 124 us
  waiting for transfers between devices  55.3 us (44%)
  starting transfers between devices  54.4 us (44%)
  local copies, waits for them, and re-layouts  6.35 us (5%)
  Pallas kernels  6.35 us (5%)
  other arithmetic  1.78 us (1%)
    all_to_all x4, starting transfers between devices, exchange(): return lax.all_to_all(payload, axis, 0, 0)  31.2 us
    ppermute x2, waiting for transfers between devices, turn(): lax.ppermute(payload, axes, direct)  27.5 us
    all_to_all x4, waiting for transfers between devices, exchange(): return lax.all_to_all(payload, axis, 0, 0)  19.6 us
    ppermute x2, starting transfers between devices, turn(): lax.ppermute(payload, axes, direct)  16.7 us
    ppermute x2, waiting for transfers between devices, turn(): lax.ppermute(payload, axes, crossed)  8.17 us
    ppermute x2, starting transfers between devices, turn(): lax.ppermute(payload, axes, crossed)  6.51 us
    pallas_call x1, Pallas kernels, finish(): pl.pallas_call(body, out_shape=jax.ShapeDtypeStruct(hamiltonian.shape, jn...  6.35 us
  transfers between devices with their start and end apart: 8, of which 6 were waited for; matrix products, arithmetic and copies ran while one was open for 4% of the time, Pallas kernels for 0%

profile of v1, /device:TPU:201, one launch (start us, length us, event | category | flops | bytes accessed | tf_op | source)
XLA Modules:
  0.0 124.4 jit_solution(4612580723361819250)
XLA Ops:
  0.0 0.9 slice.24
  0.9 0.7 reshape.18
  1.6 8.5 %all-to-all-start = ((f32[16,4,384]{2,1,0:T(4,128)}), f32[16,4,384]{2,1,0:T(4,128)S(1)}, u32[]{:S(2)}, u32[]{:S(2)}) async-start(f32[16,4,384]{2,1,0:T(4,128)} %reshape.18), calls=%async_computation | async-start | bytes 196608 | tf_op jit(solution)/shard_map/all_to_all | solution.py:92
  10.0 0.8 slice.26
  10.9 4.8 %all-to-all-done = f32[16,4,384]{2,1,0:T(4,128)S(1)} async-done(((f32[16,4,384]{2,1,0:T(4,128)}), f32[16,4,384]{2,1,0:T(4,128)S(1)}, u32[]{:S(2)}, u32[]{:S(2)}) %all-to-all-start) | async-done | bytes 98336 | tf_op jit(solution)/shard_map/all_to_all | solution.py:92
  15.8 0.9 reshape.21
  16.7 9.6 %all-to-all-start.2 = ((f32[32,1,1024]{2,1,0:T(1,128)}), f32[32,1,1024]{2,1,0:T(1,128)S(1)}, u32[]{:S(2)}, u32[]{:S(2)}) async-start(f32[32,1,1024]{2,1,0:T(1,128)} %reshape.21), calls=%async_computation.2 | async-start | bytes 262144 | tf_op jit(solution)/shard_map/all_to_all | solution.py:92
  26.3 0.0 copy-start
  26.3 9.5 %all-to-all-done.2 = f32[32,1,1024]{2,1,0:T(1,128)S(1)} async-done(((f32[32,1,1024]{2,1,0:T(1,128)}), f32[32,1,1024]{2,1,0:T(1,128)S(1)}, u32[]{:S(2)}, u32[]{:S(2)}) %all-to-all-start.2) | async-done | bytes 131104 | tf_op jit(solution)/shard_map/all_to_all | solution.py:92
  35.8 0.7 broadcast_in_dim.6
  36.5 7.6 %all-to-all-start.1 = ((f32[16,2,4,384]{3,2,1,0:T(4,128)}), f32[16,2,4,384]{3,2,1,0:T(4,128)S(1)}, u32[]{:S(2)}, u32[]{:S(2)}) async-start(f32[16,2,4,384]{3,2,1,0:T(4,128)} %broadcast_in_dim.6), calls=%async_computation.1 | async-start | bytes 393216 | tf_op jit(solution)/shard_map/all_to_all | solution.py:92
  44.1 0.5 broadcast.3
  44.6 0.8 reduce
  45.5 0.2 reshape.22
  45.7 0.1 broadcast_bitcast_fusion
  45.8 0.9 reshape.23
  46.7 5.3 %all-to-all-done.1 = f32[16,2,4,384]{3,2,1,0:T(4,128)S(1)} async-done(((f32[16,2,4,384]{3,2,1,0:T(4,128)}), f32[16,2,4,384]{3,2,1,0:T(4,128)S(1)}, u32[]{:S(2)}, u32[]{:S(2)}) %all-to-all-start.1) | async-done | bytes 196640 | tf_op jit(solution)/shard_map/all_to_all | solution.py:92
  52.0 5.5 %all-to-all-start.3 = ((f32[16,1,2048]{2,1,0:T(1,128)}), f32[16,1,2048]{2,1,0:T(1,128)S(1)}, u32[]{:S(2)}, u32[]{:S(2)}) async-start(f32[16,1,2048]{2,1,0:T(1,128)} %reshape.23), calls=%async_computation.3 | async-start | bytes 262144 | tf_op jit(solution)/shard_map/all_to_all | solution.py:92
  57.5 0.0 copy-done
  57.5 2.0 %collective-permute-start.1 = (f32[128,384]{1,0:T(8,128)S(1)}, f32[128,384]{1,0:T(8,128)S(1)}, u32[]{:S(2)}, u32[]{:S(2)}) collective-permute-start(f32[128,384]{1,0:T(8,128)S(1)} %copy-done), channel_id=1, source_target_pairs={{0,1},{1,33},{2,65},{3,97},{4,129},{5,161},{6,193},{7,225},{8,257}... | collective-permute-start | bytes 589832 | tf_op jit(solution)/shard_map/ppermute | solution.py:114
  59.4 8.9 %collective-permute-start = (f32[128,384]{1,0:T(8,128)S(1)}, f32[128,384]{1,0:T(8,128)S(1)}, u32[]{:S(2)}, u32[]{:S(2)}) collective-permute-start(f32[128,384]{1,0:T(8,128)S(1)} %copy-done), channel_id=1, source_target_pairs={{0,0},{1,32},{2,64},{3,96},{4,128},{5,160},{6,192},{7,224},{8,256}... | collective-permute-start | bytes 589832 | tf_op jit(solution)/shard_map/ppermute | solution.py:114
  68.3 0.1 pad_add_fusion.place
  68.4 0.1 reshape.19.hj_ref
  68.5 4.6 %collective-permute-start.3 = (f32[128,384]{1,0:T(8,128)S(1)}, f32[128,384]{1,0:T(8,128)S(1)}, u32[]{:S(2)}, u32[]{:S(2)}) collective-permute-start(f32[128,384]{1,0:T(8,128)S(1)} %reshape.19.hj_ref), channel_id=1, source_target_pairs={{0,1},{1,33},{2,65},{3,97},{4,129},{5,161},{6,193},{7,225},{8,257}... | collective-permute-start | bytes 589832 | tf_op jit(solution)/shard_map/ppermute | solution.py:114
  73.1 7.8 %collective-permute-start.2 = (f32[128,384]{1,0:T(8,128)S(1)}, f32[128,384]{1,0:T(8,128)S(1)}, u32[]{:S(2)}, u32[]{:S(2)}) collective-permute-start(f32[128,384]{1,0:T(8,128)S(1)} %reshape.19.hj_ref), channel_id=1, source_target_pairs={{0,0},{1,32},{2,64},{3,96},{4,128},{5,160},{6,192},{7,224},{8,256}... | collective-permute-start | bytes 589832 | tf_op jit(solution)/shard_map/ppermute | solution.py:114
  80.9 0.0 all-to-all-done.3
  80.9 0.8 reduce.1
  81.8 0.0 copy-start.1
  81.8 0.2 reshape.24
  82.1 0.1 squeeze.9.corner_ref
  82.2 0.1 squeeze.8.factor_ref
  82.3 8.2 %collective-permute-done.1.rb_ref = f32[128,384]{1,0:T(8,128)S(1)} collective-permute-done((f32[128,384]{1,0:T(8,128)S(1)}, f32[128,384]{1,0:T(8,128)S(1)}, u32[]{:S(2)}, u32[]{:S(2)}) %collective-permute-start.1) | collective-permute-done | bytes 196640 | tf_op jit(solution)/shard_map/ppermute | solution.py:114
  90.5 24.4 %collective-permute-done.ra_ref = f32[128,384]{1,0:T(8,128)S(1)} collective-permute-done((f32[128,384]{1,0:T(8,128)S(1)}, f32[128,384]{1,0:T(8,128)S(1)}, u32[]{:S(2)}, u32[]{:S(2)}) %collective-permute-start) | collective-permute-done | bytes 196640 | tf_op jit(solution)/shard_map/ppermute | solution.py:114
  114.9 0.0 collective-permute-done.3.hb_ref
  114.9 3.1 %collective-permute-done.2.ha_ref = f32[128,384]{1,0:T(8,128)S(1)} collective-permute-done((f32[128,384]{1,0:T(8,128)S(1)}, f32[128,384]{1,0:T(8,128)S(1)}, u32[]{:S(2)}, u32[]{:S(2)}) %collective-permute-start.2) | collective-permute-done | bytes 196640 | tf_op jit(solution)/shard_map/ppermute | solution.py:114
  118.0 0.0 copy-done.1
  118.0 6.4 %shard_map.28 = f32[768,384]{1,0:T(8,128)} custom-call(s32[2]{0:T(128)S(1)} %pad_add_fusion.place, f32[768,384]{1,0:T(8,128)S(1)} %copy-done.1, f32[128,384]{1,0:T(8,128)S(1)} %copy-done, f32[128,384]{1,0:T(8,128)S(1)} %reshape.19.hj_ref, f32[128,384]{1,0:T(8,128)S(1)} %collective-permute-done.ra_ref, f32[128,384]{1,0:T(8,128)S(1)} %collective-permute-done.1.rb_ref, ...), custom_call_target="tpu_custom_call" | custom-call | flops 1000000000 | bytes 5000000 | tf_op jit(solution)/shard_map/pallas_call | solution.py:81
  (12 shorter events, 0.1 us)
Async XLA Ops:
  1.6 14.1 %all-to-all-start = ((f32[16,4,384]{2,1,0:T(4,128)}), f32[16,4,384]{2,1,0:T(4,128)S(1)}, u32[]{:S(2)}, u32[]{:S(2)}) async-start(f32[16,4,384]{2,1,0:T(4,128)} %reshape.18), calls=%async_computation | async-start | bytes 196608 | tf_op jit(solution)/shard_map/all_to_all | solution.py:92
  16.7 19.1 %all-to-all-start.2 = ((f32[32,1,1024]{2,1,0:T(1,128)}), f32[32,1,1024]{2,1,0:T(1,128)S(1)}, u32[]{:S(2)}, u32[]{:S(2)}) async-start(f32[32,1,1024]{2,1,0:T(1,128)} %reshape.21), calls=%async_computation.2 | async-start | bytes 262144 | tf_op jit(solution)/shard_map/all_to_all | solution.py:92
  26.3 31.2 %copy-start = (f32[128,384]{1,0:T(8,128)S(1)}, f32[128,384]{1,0:T(8,128)}, u32[]{:S(2)}) copy-start(f32[128,384]{1,0:T(8,128)} %rj_ref.1) | copy-start | bytes 589828
  36.5 15.5 %all-to-all-start.1 = ((f32[16,2,4,384]{3,2,1,0:T(4,128)}), f32[16,2,4,384]{3,2,1,0:T(4,128)S(1)}, u32[]{:S(2)}, u32[]{:S(2)}) async-start(f32[16,2,4,384]{3,2,1,0:T(4,128)} %broadcast_in_dim.6), calls=%async_computation.1 | async-start | bytes 393216 | tf_op jit(solution)/shard_map/all_to_all | solution.py:92
  52.0 28.9 %all-to-all-start.3 = ((f32[16,1,2048]{2,1,0:T(1,128)}), f32[16,1,2048]{2,1,0:T(1,128)S(1)}, u32[]{:S(2)}, u32[]{:S(2)}) async-start(f32[16,1,2048]{2,1,0:T(1,128)} %reshape.23), calls=%async_computation.3 | async-start | bytes 262144 | tf_op jit(solution)/shard_map/all_to_all | solution.py:92
  57.5 33.0 %collective-permute-start.1 = (f32[128,384]{1,0:T(8,128)S(1)}, f32[128,384]{1,0:T(8,128)S(1)}, u32[]{:S(2)}, u32[]{:S(2)}) collective-permute-start(f32[128,384]{1,0:T(8,128)S(1)} %copy-done), channel_id=1, source_target_pairs={{0,1},{1,33},{2,65},{3,97},{4,129},{5,161},{6,193},{7,225},{8,257}... | collective-permute-start | bytes 589832 | tf_op jit(solution)/shard_map/ppermute | solution.py:114
  59.4 55.5 %collective-permute-start = (f32[128,384]{1,0:T(8,128)S(1)}, f32[128,384]{1,0:T(8,128)S(1)}, u32[]{:S(2)}, u32[]{:S(2)}) collective-permute-start(f32[128,384]{1,0:T(8,128)S(1)} %copy-done), channel_id=1, source_target_pairs={{0,0},{1,32},{2,64},{3,96},{4,128},{5,160},{6,192},{7,224},{8,256}... | collective-permute-start | bytes 589832 | tf_op jit(solution)/shard_map/ppermute | solution.py:114
  68.5 46.4 %collective-permute-start.3 = (f32[128,384]{1,0:T(8,128)S(1)}, f32[128,384]{1,0:T(8,128)S(1)}, u32[]{:S(2)}, u32[]{:S(2)}) collective-permute-start(f32[128,384]{1,0:T(8,128)S(1)} %reshape.19.hj_ref), channel_id=1, source_target_pairs={{0,1},{1,33},{2,65},{3,97},{4,129},{5,161},{6,193},{7,225},{8,257}... | collective-permute-start | bytes 589832 | tf_op jit(solution)/shard_map/ppermute | solution.py:114
  73.1 45.0 %collective-permute-start.2 = (f32[128,384]{1,0:T(8,128)S(1)}, f32[128,384]{1,0:T(8,128)S(1)}, u32[]{:S(2)}, u32[]{:S(2)}) collective-permute-start(f32[128,384]{1,0:T(8,128)S(1)} %reshape.19.hj_ref), channel_id=1, source_target_pairs={{0,0},{1,32},{2,64},{3,96},{4,128},{5,160},{6,192},{7,224},{8,256}... | collective-permute-start | bytes 589832 | tf_op jit(solution)/shard_map/ppermute | solution.py:114
  81.8 36.3 %copy-start.1 = (f32[768,384]{1,0:T(8,128)S(1)}, f32[768,384]{1,0:T(8,128)}, u32[]{:S(2)}) copy-start(f32[768,384]{1,0:T(8,128)} %h_ref.1) | copy-start | bytes 3538948

commit v2 on v1

--- a/solution.py
+++ b/solution.py
@@ -37,27 +37,43 @@
     return total - dot(total, dot(couple, total))
 
 
-def body(
-    place, h_ref, rj_ref, hj_ref, ra_ref, rb_ref, ha_ref, hb_ref, factor_ref, corner_ref, out_ref
-):
+def body(place, h_ref, rj_ref, hj_ref, turned_ref, corner_ref, out_ref):
     grid_row, grid_col = place[0], place[1]
-    inverse = wide_inverse(factor_ref[...])
-    result = dot(inner(inverse, corner_ref[...]), inverse)
+    corners = [corner_ref[:, part].reshape(WIDE, WIDE) for part in (0, 1)]
+    corner = jnp.concatenate([piece[:, :BLOCK] for piece in corners], axis=1)
+    inverse = wide_inverse(jnp.concatenate([piece[:, BLOCK:] for piece in corners], axis=1))
+    result = dot(inner(inverse, corner), inverse)
     width = rj_ref.shape[1]
+    r_own, h_own = rj_ref[...], hj_ref[...]
     weights = jnp.concatenate([inverse.T, -0.5 * result], axis=1)
-    r_own, h_own = rj_ref[...], hj_ref[...]
     z_own = dot(weights, jnp.concatenate([h_own, r_own], axis=0))
     right = jnp.concatenate([z_own, r_own], axis=0)
+    across = jnp.concatenate([-0.5 * result.T, inverse], axis=0)
+    holders, twice, _ = turned_ref.shape
+    slab = twice // 2
+    r_pieces = turned_ref[:, :slab].reshape(2, WIDE, width)
+    h_rows = jnp.concatenate(
+        [
+            turned_ref[:, slab:, part * WIDE : (part + 1) * WIDE].reshape(holders, 1, slab, WIDE)
+            for part in range(width // WIDE)
+        ],
+        axis=1,
+    ).reshape(-1, WIDE)
     lane = lax.broadcasted_iota(jnp.int32, (BLOCK, width), 1)
     inside = (lane >= BLOCK) | (grid_col >= 2)
-    parity = lax.rem(grid_col, 2)
-    for order, (r_piece, h_piece) in enumerate(((ra_ref, ha_ref), (rb_ref, hb_ref))):
-        r_rows = r_piece[...]
-        z_rows = dot(weights, jnp.concatenate([h_piece[...], r_rows], axis=0))
-        change = inner(jnp.concatenate([r_rows, z_rows], axis=0), right)
-        section = parity if order == 0 else 1 - parity
+    for section in range(2):
+        r_cols = r_pieces[section].T
+        h_cols = jnp.concatenate(
+            [
+                h_rows[(2 * m + section) * BLOCK : (2 * m + section + 1) * BLOCK]
+                for m in range(width // BLOCK)
+            ],
+            axis=0,
+        )
+        z_cols = dot(jnp.concatenate([r_cols, h_cols], axis=1), across)
+        change = dot(jnp.concatenate([r_cols, z_cols], axis=1), right)
         for m in range(width // BLOCK):
-            rows = pl.ds(pl.multiple_of((2 * m + section) * BLOCK, BLOCK), BLOCK)
+            rows = slice((2 * m + section) * BLOCK, (2 * m + section + 1) * BLOCK)
             part = change[m * BLOCK : (m + 1) * BLOCK]
             out_ref[rows, :] = h_ref[rows, :] - jnp.where(inside, part, 0.0)
 
@@ -99,35 +115,32 @@
 def per_device(hamiltonian, factor_rows):
     grid_rows, grid_cols = lax.axis_size("row"), lax.axis_size("col")
     row_index, col_index = lax.axis_index("row"), lax.axis_index("col")
-    width = hamiltonian.shape[1]
-    slab = BLOCK // grid_rows
+    height, width = hamiltonian.shape
+    slab = WIDE // grid_rows
 
-    def turn(payload):
-        direct, crossed = [], []
-        for r in range(grid_rows):
-            for c in range(grid_cols):
-                source = r * grid_cols + c
-                row, section = c % grid_rows, c // grid_rows
-                direct.append((source, row * grid_cols + 2 * r + section))
-                crossed.append((source, row * grid_cols + 2 * r + 1 - section))
-        axes = ("row", "col")
-        return lax.ppermute(payload, axes, direct), lax.ppermute(payload, axes, crossed)
+    top = hamiltonian[:BLOCK].reshape(grid_rows // 2, slab, width)
+    top = exchange(jnp.concatenate([top, top]), "row")
+    h_slab = jnp.where(row_index < grid_rows // 2, top[0], top[1])
+    side = hamiltonian[:, :BLOCK].reshape(grid_cols, height // grid_cols, BLOCK)
+    side = exchange(side, "col")
+    h_share = jnp.concatenate([side[0], side[1]], axis=1)
+    h_share = h_share.reshape(width // WIDE, slab, WIDE)
+    r_slab = lax.dynamic_slice_in_dim(factor_rows, row_index * slab, slab, 0)
+    pairs = [
+        (r * grid_cols + c, (c % grid_rows) * grid_cols + grid_rows * (c // grid_rows) + r)
+        for r in range(grid_rows)
+        for c in range(grid_cols)
+    ]
+    r_share = lax.ppermute(r_slab, ("row", "col"), pairs)
 
-    ra, rb = turn(factor_rows)
-    top = hamiltonian[:BLOCK].reshape(grid_rows, slab, width)
-    mine = exchange(top, "row")[:2]
-    panel = offer(mine, "row", grid_rows)
-    panel = panel.transpose(1, 0, 2, 3).reshape(WIDE, width)
-    lead = factor_rows[:, :BLOCK].reshape(2, grid_rows, slab, BLOCK)
-    lead = lax.dynamic_index_in_dim(lead, row_index, 1, keepdims=False)
-    pieces = offer(jnp.stack([lead, mine[:, :, :BLOCK]]), "col", grid_cols)[:2]
-    pieces = offer(pieces, "row", grid_rows)
-    pieces = pieces.transpose(2, 3, 0, 4, 1, 5).reshape(2, WIDE, WIDE)
-    ha, hb = turn(panel)
+    corner = jnp.concatenate([h_slab[:, :BLOCK], r_slab[:, :BLOCK]], axis=1)
+    corner = offer(corner, "col", grid_cols)[:2]
+    panel = offer(h_slab, "row", grid_rows).reshape(WIDE, width)
+    share = jnp.concatenate([r_share, jnp.concatenate(list(h_share), axis=1)], axis=0)
+    turned = lax.all_gather(share, "col")
+    corner = offer(corner, "row", grid_rows)
     place = jnp.stack([row_index, col_index])
-    return finish(
-        place, hamiltonian, factor_rows, panel, ra, rb, ha, hb, pieces[0], pieces[1]
-    )
+    return finish(place, hamiltonian, factor_rows, panel, turned, corner)
 
 
 def solution(mesh):

time: 125 us -> 133 us (1.064)
  the two profiles are of different devices: /device:TPU:201 before, /device:TPU:2 now
where the time goes in v2:
time: 133 us
  blocking collectives  48.5 us (36%)
  starting transfers between devices  36.1 us (27%)
  waiting for transfers between devices  33.7 us (25%)
  Pallas kernels  7.26 us (5%)
  local copies, waits for them, and re-layouts  4.62 us (3%)
  other arithmetic  2.18 us (2%)
    all_gather x1, blocking collectives, per_device(): turned = lax.all_gather(share, 'col')  48.5 us
    all_to_all x5, waiting for transfers between devices, exchange(): return lax.all_to_all(payload, axis, 0, 0)  33.7 us
    all_to_all x5, starting transfers between devices, exchange(): return lax.all_to_all(payload, axis, 0, 0)  33.4 us
    pallas_call x1, Pallas kernels, finish(): pl.pallas_call(body, out_shape=jax.ShapeDtypeStruct(hamiltonian.shape, jn...  7.26 us
    ppermute x1, starting transfers between devices, per_device(): r_share = lax.ppermute(r_slab, ('row', 'col'), pairs)  2.77 us
  transfers between devices with their start and end apart: 6, of which 4 were waited for; matrix products, arithmetic and copies ran while one was open for 3% of the time, Pallas kernels for 0%

profile of v2, /device:TPU:2, one launch (start us, length us, event | category | flops | bytes accessed | tf_op | source)
XLA Modules:
  0.0 132.6 jit_solution(3016796591850580817)
XLA Ops:
  0.0 0.0 slice-start
  0.0 1.0 slice_bitcast_fusion
  1.0 0.0 copy-start.1
  1.0 0.7 pad_maximum_fusion
  1.7 10.4 %all-to-all-start = ((f32[16,8,384]{2,1,0:T(8,128)}), f32[16,8,384]{2,1,0:T(8,128)S(1)}, u32[]{:S(2)}, u32[]{:S(2)}) async-start(f32[16,8,384]{2,1,0:T(8,128)} %pad_maximum_fusion), calls=%async_computation | async-start | bytes 393216 | tf_op jit(solution)/shard_map/all_to_all | solution.py:108
  12.1 0.0 slice-done
  12.1 0.9 reshape.24
  13.0 9.0 %all-to-all-done = f32[16,8,384]{2,1,0:T(8,128)S(1)} async-done(((f32[16,8,384]{2,1,0:T(8,128)}), f32[16,8,384]{2,1,0:T(8,128)S(1)}, u32[]{:S(2)}, u32[]{:S(2)}) %all-to-all-start) | async-done | bytes 196640 | tf_op jit(solution)/shard_map/all_to_all | solution.py:108
  22.1 10.3 %all-to-all-start.2 = ((f32[32,1,1536]{2,1,0:T(1,128)}), f32[32,1,1536]{2,1,0:T(1,128)S(1)}, u32[]{:S(2)}, u32[]{:S(2)}) async-start(f32[32,1,1536]{2,1,0:T(1,128)} %reshape.24), calls=%async_computation.2 | async-start | bytes 393216 | tf_op jit(solution)/shard_map/all_to_all | solution.py:108
  32.3 0.0 copy-done.1
  32.4 0.1 pad_maximum_fusion.1
  32.5 10.6 %all-to-all-done.2 = f32[32,1,1536]{2,1,0:T(1,128)S(1)} async-done(((f32[32,1,1536]{2,1,0:T(1,128)}), f32[32,1,1536]{2,1,0:T(1,128)S(1)}, u32[]{:S(2)}, u32[]{:S(2)}) %all-to-all-start.2) | async-done | bytes 196640 | tf_op jit(solution)/shard_map/all_to_all | solution.py:108
  43.1 0.7 broadcast_in_dim.10
  43.7 5.6 %all-to-all-start.3 = ((f32[32,8,128]{2,1,0:T(8,128)}), f32[32,8,128]{2,1,0:T(8,128)S(1)}, u32[]{:S(2)}, u32[]{:S(2)}) async-start(f32[32,8,128]{2,1,0:T(8,128)} %broadcast_in_dim.10), calls=%async_computation.3 | async-start | bytes 262144 | tf_op jit(solution)/shard_map/all_to_all | solution.py:108
  49.4 2.8 %collective-permute-start = (f32[8,384]{1,0:T(8,128)S(1)}, f32[8,384]{1,0:T(8,128)S(1)}, u32[]{:S(2)}, u32[]{:S(2)}) collective-permute-start(f32[8,384]{1,0:T(8,128)S(1)} %constant_dynamic-slice_fusion.1), channel_id=1, source_target_pairs={{0,0},{1,32},{2,64},{3,96},{4,128},{5,160},{6,192},{7,224},{8,256}... | collective-permute-start | bytes 36872 | tf_op jit(solution)/shard_map/ppermute | solution.py:134
  52.2 6.3 %all-to-all-done.3 = f32[32,8,128]{2,1,0:T(8,128)S(1)} async-done(((f32[32,8,128]{2,1,0:T(8,128)}), f32[32,8,128]{2,1,0:T(8,128)S(1)}, u32[]{:S(2)}, u32[]{:S(2)}) %all-to-all-start.3) | async-done | bytes 131104 | tf_op jit(solution)/shard_map/all_to_all | solution.py:108
  58.5 0.7 broadcast_in_dim.9
  59.2 3.5 %all-to-all-start.1 = ((f32[16,8,384]{2,1,0:T(8,128)}), f32[16,8,384]{2,1,0:T(8,128)S(1)}, u32[]{:S(2)}, u32[]{:S(2)}) async-start(f32[16,8,384]{2,1,0:T(8,128)} %broadcast_in_dim.9), calls=%async_computation.1 | async-start | bytes 393216 | tf_op jit(solution)/shard_map/all_to_all | solution.py:108
  62.7 0.1 pad_add_fusion.place
  62.8 0.5 broadcast.16
  63.3 0.0 copy-start
  63.3 1.2 reduce
  64.5 0.1 reshape.25
  64.7 0.1 fusion.4
  64.7 7.8 %all-to-all-done.1 = f32[16,8,384]{2,1,0:T(8,128)S(1)} async-done(((f32[16,8,384]{2,1,0:T(8,128)}), f32[16,8,384]{2,1,0:T(8,128)S(1)}, u32[]{:S(2)}, u32[]{:S(2)}) %all-to-all-start.1) | async-done | bytes 196640 | tf_op jit(solution)/shard_map/all_to_all | solution.py:108
  72.5 0.7 broadcast_in_dim.11
  73.2 3.5 %all-to-all-start.4 = ((f32[16,2,8,128]{3,2,1,0:T(8,128)}), f32[16,2,8,128]{3,2,1,0:T(8,128)S(1)}, u32[]{:S(2)}, u32[]{:S(2)}) async-start(f32[16,2,8,128]{3,2,1,0:T(8,128)} %broadcast_in_dim.11), calls=%async_computation.4 | async-start | bytes 262144 | tf_op jit(solution)/shard_map/all_to_all | solution.py:108
  76.7 0.0 collective-permute-done
  76.7 0.1 fusion.1
  76.8 48.5 %all-gather = f32[512,384]{1,0:T(8,128)S(1)} all-gather(f32[16,384]{1,0:T(8,128)S(1)} %fusion.1), channel_id=2, replica_groups=mesh['row'=16,'col'=32] {'col'}, dimensions={0}, use_global_device_ids=true | all-gather | bytes 811008 | tf_op jit(solution)/shard_map/all_gather | solution.py:140
  125.3 0.0 all-to-all-done.4.corner_ref
  125.3 0.0 copy-done
  125.3 7.3 %shard_map.28 = f32[768,384]{1,0:T(8,128)} custom-call(s32[2]{0:T(128)S(1)} %pad_add_fusion.place, f32[768,384]{1,0:T(8,128)S(1)} %copy-done, f32[128,384]{1,0:T(8,128)S(1)} %copy-done.1, f32[128,384]{1,0:T(8,128)S(1)} %bitcast.15, f32[32,16,384]{2,1,0:T(8,128)S(1)} %bitcast.13, f32[16,2,8,128]{3,2,1,0:T(8,128)S(1)} %all-to-all-done.4.corner_ref), custom_call_target="tpu_custom_call" | custom-call | flops 1000000000 | bytes 5000000 | tf_op jit(solution)/shard_map/pallas_call | solution.py:97
  (6 shorter events, 0.0 us)
Async XLA Ops:
  0.0 12.1 %slice-start = ((f32[768,384]{1,0:T(8,128)}), f32[768,64]{1,0:T(8,128)S(1)}, s32[]{:S(2)}) async-start(f32[768,384]{1,0:T(8,128)} %h_ref.1), calls=%async_computation.5 | async-start | bytes 786432 | tf_op jit(solution)/shard_map/slice | solution.py:124
  1.0 31.3 %copy-start.1 = (f32[128,384]{1,0:T(8,128)S(1)}, f32[128,384]{1,0:T(8,128)}, u32[]{:S(2)}) copy-start(f32[128,384]{1,0:T(8,128)} %rj_ref.1) | copy-start | bytes 589828
  1.7 20.4 %all-to-all-start = ((f32[16,8,384]{2,1,0:T(8,128)}), f32[16,8,384]{2,1,0:T(8,128)S(1)}, u32[]{:S(2)}, u32[]{:S(2)}) async-start(f32[16,8,384]{2,1,0:T(8,128)} %pad_maximum_fusion), calls=%async_computation | async-start | bytes 393216 | tf_op jit(solution)/shard_map/all_to_all | solution.py:108
  22.1 21.0 %all-to-all-start.2 = ((f32[32,1,1536]{2,1,0:T(1,128)}), f32[32,1,1536]{2,1,0:T(1,128)S(1)}, u32[]{:S(2)}, u32[]{:S(2)}) async-start(f32[32,1,1536]{2,1,0:T(1,128)} %reshape.24), calls=%async_computation.2 | async-start | bytes 393216 | tf_op jit(solution)/shard_map/all_to_all | solution.py:108
  43.7 14.8 %all-to-all-start.3 = ((f32[32,8,128]{2,1,0:T(8,128)}), f32[32,8,128]{2,1,0:T(8,128)S(1)}, u32[]{:S(2)}, u32[]{:S(2)}) async-start(f32[32,8,128]{2,1,0:T(8,128)} %broadcast_in_dim.10), calls=%async_computation.3 | async-start | bytes 262144 | tf_op jit(solution)/shard_map/all_to_all | solution.py:108
  49.4 27.3 %collective-permute-start = (f32[8,384]{1,0:T(8,128)S(1)}, f32[8,384]{1,0:T(8,128)S(1)}, u32[]{:S(2)}, u32[]{:S(2)}) collective-permute-start(f32[8,384]{1,0:T(8,128)S(1)} %constant_dynamic-slice_fusion.1), channel_id=1, source_target_pairs={{0,0},{1,32},{2,64},{3,96},{4,128},{5,160},{6,192},{7,224},{8,256}... | collective-permute-start | bytes 36872 | tf_op jit(solution)/shard_map/ppermute | solution.py:134
  59.2 13.4 %all-to-all-start.1 = ((f32[16,8,384]{2,1,0:T(8,128)}), f32[16,8,384]{2,1,0:T(8,128)S(1)}, u32[]{:S(2)}, u32[]{:S(2)}) async-start(f32[16,8,384]{2,1,0:T(8,128)} %broadcast_in_dim.9), calls=%async_computation.1 | async-start | bytes 393216 | tf_op jit(solution)/shard_map/all_to_all | solution.py:108
  63.3 62.0 %copy-start = (f32[768,384]{1,0:T(8,128)S(1)}, f32[768,384]{1,0:T(8,128)}, u32[]{:S(2)}) copy-start(f32[768,384]{1,0:T(8,128)} %h_ref.1) | copy-start | bytes 3538948
  73.2 52.1 %all-to-all-start.4 = ((f32[16,2,8,128]{3,2,1,0:T(8,128)}), f32[16,2,8,128]{3,2,1,0:T(8,128)S(1)}, u32[]{:S(2)}, u32[]{:S(2)}) async-start(f32[16,2,8,128]{3,2,1,0:T(8,128)} %broadcast_in_dim.11), calls=%async_computation.4 | async-start | bytes 262144 | tf_op jit(solution)/shard_map/all_to_all | solution.py:108

commit v3 on v2

v3 whole, which is shorter than its diff:
```python
import jax
import jax.numpy as jnp
from jax import lax
from jax.experimental import pallas as pl
from jax.experimental.pallas import tpu as pltpu
from jax.sharding import PartitionSpec as P

BLOCK = 64
WIDE = 2 * BLOCK
EXACT = lax.Precision.HIGHEST


def dot(left, right):
    return jnp.dot(left, right, precision=EXACT, preferred_element_type=jnp.float32)


def inner(left, right):
    return lax.dot_general(
        left, right, (((0,), (0,)), ((), ())), precision=EXACT, preferred_element_type=jnp.float32
    )


def wide_inverse(factor):
    row = lax.broadcasted_iota(jnp.int32, (WIDE, WIDE), 0)
    col = lax.broadcasted_iota(jnp.int32, (WIDE, WIDE), 1)
    on_diag = jnp.where(row == col, factor, 0.0)
    diag_col = jnp.sum(on_diag, axis=1, keepdims=True)
    diag_row = jnp.sum(on_diag, axis=0, keepdims=True)
    same = (row < BLOCK) == (col < BLOCK)
    power = jnp.where((row < col) & same, -factor / diag_col, 0.0)
    total = jnp.where(row == col, 1.0, power)
    for _ in range(5):
        power = dot(power, power)
        total = total + dot(total, power)
    total = total / diag_row
    couple = jnp.where((row < BLOCK) & (col >= BLOCK), factor, 0.0)
    return total - dot(total, dot(couple, total))


def beside(left, right):
    return jnp.concatenate([left, right], axis=1)


def owner_of(block):
    k = block // 4
    return (block + k) % 4, k


def pack_columns(h_ref, r_ref, out_ref):
    h_cols, r_cols = h_ref[:, :BLOCK], r_ref[:, :BLOCK]
    first = h_cols[: 4 * BLOCK]
    second = jnp.concatenate([h_cols[7 * BLOCK : 8 * BLOCK], h_cols[4 * BLOCK : 7 * BLOCK]])
    third = jnp.concatenate([h_cols[10 * BLOCK :], h_cols[8 * BLOCK : 10 * BLOCK]])
    corner = jnp.concatenate([h_cols[:BLOCK], h_cols[:BLOCK], r_cols])
    out_ref[:, 0] = beside(first, second).reshape(-1, 8, WIDE)
    out_ref[:, 1] = beside(third, corner).reshape(-1, 8, WIDE)


def pack_share(halves_ref, out_ref):
    for slot in range(2):
        left, right = halves_ref[0, slot], halves_ref[1, slot]
        low = beside(left[:, :BLOCK], right[:, :BLOCK])
        high = beside(left[:, BLOCK:], right[:, BLOCK:])
        for row in range(out_ref.shape[0]):
            out_ref[row, 2 * slot] = low
            out_ref[row, 2 * slot + 1] = high


def pack_gather(place, all_ref, r_ref, out_ref):
    grid_row, grid_col = place[0], place[1]
    grid_rows, grid_cols = all_ref.shape[0], out_ref.shape[0]
    own = all_ref[grid_row]
    corner_from = jnp.minimum(grid_col // 8, 1)
    corner = all_ref[corner_from, 3]
    parity = lax.rem(grid_col // 8, 2)
    for col in range(grid_cols):
        section = col // grid_rows
        lead = jnp.where(parity == section, 0, 1)
        for k in range(3):
            out_ref[col, k] = own[k]
        out_ref[col, 3] = all_ref[col % grid_rows, lead]
        out_ref[col, 4] = all_ref[col % grid_rows, 2]
        out_ref[col, 5] = corner
        for k in range(3):
            out_ref[col, 6 + k] = r_ref[:, k * WIDE : (k + 1) * WIDE]


def body(place, h_ref, rj_ref, got_ref, out_ref):
    grid_row, grid_col = place[0], place[1]
    width = rj_ref.shape[1]
    corner = got_ref[:, 5].reshape(2, WIDE, WIDE)
    inverse = wide_inverse(corner[1])
    result = dot(inner(inverse, corner[0]), inverse)
    own_section = grid_col // 16
    h_own = []
    for m in range(width // BLOCK):
        (even, k), (odd, _) = owner_of(2 * m), owner_of(2 * m + 1)
        group = jnp.where(own_section == 0, even, odd)
        slot = 4 if k == 2 else 3
        h_own.append(got_ref[pl.ds(8 * group, 8), slot].reshape(BLOCK, WIDE))
    h_own = jnp.concatenate(h_own).T
    r_own = rj_ref[...]
    weights = beside(inverse.T, -0.5 * result)
    z_own = dot(weights, jnp.concatenate([h_own, r_own], axis=0))
    right = jnp.concatenate([z_own, r_own], axis=0)
    across = jnp.concatenate([-0.5 * result.T, inverse], axis=0)
    lane = lax.broadcasted_iota(jnp.int32, (BLOCK, width), 1)
    inside = (lane >= BLOCK) | (grid_col >= 2)
    for section in range(2):
        r_piece = jnp.concatenate(
            [
                got_ref[16 * section : 16 * section + 16, 6 + k].reshape(WIDE, WIDE).T
                for k in range(width // WIDE)
            ]
        )
        h_piece = []
        for m in range(width // BLOCK):
            group, k = owner_of(2 * m + section)
            h_piece.append(got_ref[8 * group : 8 * group + 8, k].reshape(BLOCK, WIDE))
        z_piece = dot(beside(r_piece, jnp.concatenate(h_piece)), across)
        change = dot(beside(r_piece, z_piece), right)
        for m in range(width // BLOCK):
            rows = slice((2 * m + section) * BLOCK, (2 * m + section + 1) * BLOCK)
            part = change[m * BLOCK : (m + 1) * BLOCK]
            out_ref[rows, :] = h_ref[rows, :] - jnp.where(inside, part, 0.0)

    @pl.when(grid_row < 2)
    def _():
        pending = z_own - 0.5 * dot(result, r_own)
        old = h_ref[:BLOCK, :]
        first = grid_row == 0
        rest = jnp.where(first, pending[:BLOCK], pending[BLOCK:])
        lead = jnp.where(first, result[:BLOCK], result[BLOCK:])
        spread = jnp.concatenate([lead] * (width // WIDE), axis=1)
        turned = jnp.concatenate([beside(lead[:, BLOCK:], lead[:, :BLOCK])] * (width // WIDE), axis=1)
        at_zero = jnp.where(first, spread, old)
        head = jnp.where(grid_col == 0, at_zero, turned)
        out_ref[:BLOCK, :] = jnp.where(inside, rest, head)


VMEM = pl.BlockSpec(memory_space=pltpu.VMEM)
SMEM = pl.BlockSpec(memory_space=pltpu.SMEM)


def call(function, shape, specs, *operands, **more):
    return pl.pallas_call(
        function,
        out_shape=jax.ShapeDtypeStruct(shape, jnp.float32),
        in_specs=specs,
        out_specs=VMEM,
        compiler_params=pltpu.CompilerParams(vmem_limit_bytes=40 * 1024 * 1024),
        **more,
    )(*operands)


def exchange(payload, axis):
    return lax.all_to_all(payload, axis, 0, 0)


def per_device(hamiltonian, factor_rows):
    grid_rows, grid_cols = lax.axis_size("row"), lax.axis_size("col")
    row_index, col_index = lax.axis_index("row"), lax.axis_index("col")
    place = jnp.stack([row_index, col_index])

    slab = WIDE // grid_rows
    pairs = [
        (r * grid_cols + c, (c % grid_rows) * grid_cols + grid_rows * (c // grid_rows) + r)
        for r in range(grid_rows)
        for c in range(grid_cols)
    ]
    r_slab = lax.dynamic_slice_in_dim(factor_rows, row_index * slab, slab, 0)
    r_share = lax.ppermute(r_slab, ("row", "col"), pairs)

    halves = call(
        pack_columns,
        (grid_cols, 2, 8, WIDE),
        [VMEM, VMEM],
        hamiltonian[:, :WIDE],
        factor_rows[:, :WIDE],
    )
    halves = exchange(halves, "col")
    share = call(pack_share, (grid_rows, 4, 8, WIDE), [VMEM], halves[:2])
    shares = exchange(share, "row")
    offer = call(pack_gather, (grid_cols, 9, 8, WIDE), [SMEM, VMEM, VMEM], place, shares, r_share)
    got = exchange(offer, "col")
    cost = pl.CostEstimate(flops=10**9, bytes_accessed=5 * 10**6, transcendentals=0)
    return call(
        body,
        hamiltonian.shape,
        [SMEM, VMEM, VMEM, VMEM],
        place,
        hamiltonian,
        factor_rows,
        got,
        cost_estimate=cost,
    )


def solution(mesh):
    placed = (P("row", "col"), P(None, "col"))
    return jax.shard_map(
        per_device, mesh=mesh, in_specs=placed, out_specs=P("row", "col"), check_vma=False
    )
```

time: 133 us -> 92.8 us (0.70)
  the two profiles are of different devices: /device:TPU:2 before, /device:TPU:8 now
where the time goes in v3:
time: 92.8 us; the launch traced here: 92.5 us
  blocking collectives  60.1 us (65%)
  starting transfers between devices  12.7 us (14%)
  waiting for transfers between devices  8.88 us (10%)
  Pallas kernels  8.71 us (9%)
  local copies, waits for them, and re-layouts  1.89 us (2%)
    all_to_all x2, blocking collectives, exchange(): return lax.all_to_all(payload, axis, 0, 0)  60.1 us
    all_to_all x1, starting transfers between devices, exchange(): return lax.all_to_all(payload, axis, 0, 0)  10.4 us
    pallas_call x4, Pallas kernels, call(): pl.pallas_call(function, out_shape=jax.ShapeDtypeStruct(shape, jnp.float3...  8.71 us
    all_to_all x1, waiting for transfers between devices, exchange(): return lax.all_to_all(payload, axis, 0, 0)  6.27 us
    ppermute x1, waiting for transfers between devices, per_device(): r_share = lax.ppermute(r_slab, ('row', 'col'), pairs)  2.61 us
    ppermute x1, starting transfers between devices, per_device(): r_share = lax.ppermute(r_slab, ('row', 'col'), pairs)  2.31 us
  transfers between devices with their start and end apart: 2, of which 2 were waited for; matrix products, arithmetic and copies ran while one was open for 0% of the time, Pallas kernels for 0%

profile of v3, /device:TPU:8, one launch (start us, length us, event | category | flops | bytes accessed | tf_op | source)
XLA Modules:
  0.0 92.5 jit_solution(7870950814144112975)
XLA Ops:
  0.0 0.8 slice.10.r_ref
  0.8 1.0 %slice.9.h_ref = f32[768,128]{1,0:T(8,128)S(1)} slice(f32[768,384]{1,0:T(8,128)} %h_ref.1), slice={[0:768], [0:128]} | slice | bytes 786432 | tf_op jit(solution)/shard_map/slice | solution.py:178
  1.9 0.0 copy-start.1
  1.9 0.1 shard_map.28
  2.0 22.3 %all_to_all.15 = f32[32,2,8,128]{3,2,1,0:T(8,128)S(1)} all-to-all(f32[32,2,8,128]{3,2,1,0:T(8,128)S(1)} %shard_map.28), channel_id=1, replica_groups=mesh['row'=16,'col'=32] {'col'}, dimensions={0} | all-to-all | bytes 524288 | tf_op jit(solution)/shard_map/all_to_all | solution.py:157
  24.3 0.8 shard_map.29
  25.1 10.4 %all-to-all-start.1 = ((f32[16,4,8,128]{3,2,1,0:T(8,128)}), f32[16,4,8,128]{3,2,1,0:T(8,128)S(1)}, u32[]{:S(2)}, u32[]{:S(2)}) async-start(f32[16,4,8,128]{3,2,1,0:T(8,128)} %shard_map.29), calls=%async_computation.1 | async-start | bytes 524288 | tf_op jit(solution)/shard_map/all_to_all | solution.py:157
  35.5 0.0 copy-done.1
  35.5 2.3 %collective-permute-start = (f32[8,384]{1,0:T(8,128)S(1)}, f32[8,384]{1,0:T(8,128)S(1)}, u32[]{:S(2)}, u32[]{:S(2)}) collective-permute-start(f32[8,384]{1,0:T(8,128)S(1)} %constant_dynamic-slice_fusion), channel_id=1, source_target_pairs={{0,0},{1,32},{2,64},{3,96},{4,128},{5,160},{6,192},{7,224},{8,256}... | collective-permute-start | bytes 36872 | tf_op jit(solution)/shard_map/ppermute | solution.py:172
  37.9 0.1 pad_add_fusion.place
  37.9 2.6 %collective-permute-done.r_ref = f32[8,384]{1,0:T(8,128)S(1)} collective-permute-done((f32[8,384]{1,0:T(8,128)S(1)}, f32[8,384]{1,0:T(8,128)S(1)}, u32[]{:S(2)}, u32[]{:S(2)}) %collective-permute-start) | collective-permute-done | bytes 12320 | tf_op jit(solution)/shard_map/ppermute | solution.py:172
  40.5 6.3 %all-to-all-done.1.all_ref = f32[16,4,8,128]{3,2,1,0:T(8,128)S(1)} async-done(((f32[16,4,8,128]{3,2,1,0:T(8,128)}), f32[16,4,8,128]{3,2,1,0:T(8,128)S(1)}, u32[]{:S(2)}, u32[]{:S(2)}) %all-to-all-start.1) | async-done | bytes 262176 | tf_op jit(solution)/shard_map/all_to_all | solution.py:157
  46.8 0.6 shard_map.30
  47.4 0.0 copy-start
  47.4 37.9 %all_to_all.16.got_ref = f32[32,9,8,128]{3,2,1,0:T(8,128)S(1)} all-to-all(f32[32,9,8,128]{3,2,1,0:T(8,128)S(1)} %shard_map.30), channel_id=1, replica_groups=mesh['row'=16,'col'=32] {'col'}, dimensions={0} | all-to-all | bytes 2359296 | tf_op jit(solution)/shard_map/all_to_all | solution.py:157
  85.3 0.0 copy-done
  85.3 7.2 %shard_map.31 = f32[768,384]{1,0:T(8,128)} custom-call(s32[2]{0:T(128)S(1)} %pad_add_fusion.place, f32[768,384]{1,0:T(8,128)S(1)} %copy-done, f32[128,384]{1,0:T(8,128)S(1)} %copy-done.1, f32[32,9,8,128]{3,2,1,0:T(8,128)S(1)} %all_to_all.16.got_ref), custom_call_target="tpu_custom_call" | custom-call | flops 1000000000 | bytes 5000000 | tf_op jit(solution)/shard_map/pallas_call | solution.py:146
  (2 shorter events, 0.0 us)
Async XLA Ops:
  1.9 33.6 %copy-start.1 = (f32[128,384]{1,0:T(8,128)S(1)}, f32[128,384]{1,0:T(8,128)}, u32[]{:S(2)}) copy-start(f32[128,384]{1,0:T(8,128)} %rj_ref.1) | copy-start | bytes 589828
  25.1 21.7 %all-to-all-start.1 = ((f32[16,4,8,128]{3,2,1,0:T(8,128)}), f32[16,4,8,128]{3,2,1,0:T(8,128)S(1)}, u32[]{:S(2)}, u32[]{:S(2)}) async-start(f32[16,4,8,128]{3,2,1,0:T(8,128)} %shard_map.29), calls=%async_computation.1 | async-start | bytes 524288 | tf_op jit(solution)/shard_map/all_to_all | solution.py:157
  35.5 5.0 %collective-permute-start = (f32[8,384]{1,0:T(8,128)S(1)}, f32[8,384]{1,0:T(8,128)S(1)}, u32[]{:S(2)}, u32[]{:S(2)}) collective-permute-start(f32[8,384]{1,0:T(8,128)S(1)} %constant_dynamic-slice_fusion), channel_id=1, source_target_pairs={{0,0},{1,32},{2,64},{3,96},{4,128},{5,160},{6,192},{7,224},{8,256}... | collective-permute-start | bytes 36872 | tf_op jit(solution)/shard_map/ppermute | solution.py:172
  47.4 37.9 %copy-start = (f32[768,384]{1,0:T(8,128)S(1)}, f32[768,384]{1,0:T(8,128)}, u32[]{:S(2)}) copy-start(f32[768,384]{1,0:T(8,128)} %h_ref.1) | copy-start | bytes 3538948

commit v4 on v3

--- a/solution.py
+++ b/solution.py
@@ -29,10 +29,11 @@
     same = (row < BLOCK) == (col < BLOCK)
     power = jnp.where((row < col) & same, -factor / diag_col, 0.0)
     total = jnp.where(row == col, 1.0, power)
-    for _ in range(5):
-        power = dot(power, power)
-        total = total + dot(total, power)
-    total = total / diag_row
+    power = dot(power, power)
+    for _ in range(4):
+        both = dot(jnp.concatenate([power, total], axis=0), power)
+        power, total = both[:WIDE], total + both[WIDE:]
+    total = (total + dot(total, power)) / diag_row
     couple = jnp.where((row < BLOCK) & (col >= BLOCK), factor, 0.0)
     return total - dot(total, dot(couple, total))
 
@@ -66,7 +67,7 @@
             out_ref[row, 2 * slot + 1] = high
 
 
-def pack_gather(place, all_ref, r_ref, out_ref):
+def pack_gather(place, all_ref, out_ref):
     grid_row, grid_col = place[0], place[1]
     grid_rows, grid_cols = all_ref.shape[0], out_ref.shape[0]
     own = all_ref[grid_row]
@@ -81,11 +82,9 @@
         out_ref[col, 3] = all_ref[col % grid_rows, lead]
         out_ref[col, 4] = all_ref[col % grid_rows, 2]
         out_ref[col, 5] = corner
-        for k in range(3):
-            out_ref[col, 6 + k] = r_ref[:, k * WIDE : (k + 1) * WIDE]
-
-
-def body(place, h_ref, rj_ref, got_ref, out_ref):
+
+
+def body(place, h_ref, rj_ref, got_ref, ra_ref, rb_ref, out_ref):
     grid_row, grid_col = place[0], place[1]
     width = rj_ref.shape[1]
     corner = got_ref[:, 5].reshape(2, WIDE, WIDE)
@@ -106,13 +105,9 @@
     across = jnp.concatenate([-0.5 * result.T, inverse], axis=0)
     lane = lax.broadcasted_iota(jnp.int32, (BLOCK, width), 1)
     inside = (lane >= BLOCK) | (grid_col >= 2)
+    straight = lax.rem(grid_col // 8, 2) == 0
     for section in range(2):
-        r_piece = jnp.concatenate(
-            [
-                got_ref[16 * section : 16 * section + 16, 6 + k].reshape(WIDE, WIDE).T
-                for k in range(width // WIDE)
-            ]
-        )
+        r_piece = jnp.where(straight == (section == 0), ra_ref[...], rb_ref[...]).T
         h_piece = []
         for m in range(width // BLOCK):
             group, k = owner_of(2 * m + section)
@@ -162,36 +157,42 @@
     row_index, col_index = lax.axis_index("row"), lax.axis_index("col")
     place = jnp.stack([row_index, col_index])
 
-    slab = WIDE // grid_rows
-    pairs = [
-        (r * grid_cols + c, (c % grid_rows) * grid_cols + grid_rows * (c // grid_rows) + r)
-        for r in range(grid_rows)
-        for c in range(grid_cols)
-    ]
-    r_slab = lax.dynamic_slice_in_dim(factor_rows, row_index * slab, slab, 0)
-    r_share = lax.ppermute(r_slab, ("row", "col"), pairs)
+    moves = ([], [])
+    for r in range(grid_rows):
+        for c in range(grid_cols):
+            section = c // grid_rows
+            for turn in range(2):
+                pick = 2 * (r % 2) + turn
+                x, y = pick ^ section, (c + r // 2 + 2 * pick) % 8
+                moves[turn].append((r * grid_cols + c, (c % grid_rows) * grid_cols + 8 * x + y))
+    r_pieces = [lax.ppermute(factor_rows, ("row", "col"), pairs) for pairs in moves]
 
     halves = call(
         pack_columns,
         (grid_cols, 2, 8, WIDE),
-        [VMEM, VMEM],
-        hamiltonian[:, :WIDE],
-        factor_rows[:, :WIDE],
+        [pl.BlockSpec((rows, WIDE), lambda i: (0, 0)) for rows in (hamiltonian.shape[0], WIDE)],
+        hamiltonian,
+        factor_rows,
+        grid=(1,),
     )
     halves = exchange(halves, "col")
+    halves, r_first = lax.optimization_barrier((halves, r_pieces[0]))
     share = call(pack_share, (grid_rows, 4, 8, WIDE), [VMEM], halves[:2])
     shares = exchange(share, "row")
-    offer = call(pack_gather, (grid_cols, 9, 8, WIDE), [SMEM, VMEM, VMEM], place, shares, r_share)
+    shares, r_second = lax.optimization_barrier((shares, r_pieces[1]))
+    offer = call(pack_gather, (grid_cols, 6, 8, WIDE), [SMEM, VMEM], place, shares)
     got = exchange(offer, "col")
     cost = pl.CostEstimate(flops=10**9, bytes_accessed=5 * 10**6, transcendentals=0)
     return call(
         body,
         hamiltonian.shape,
-        [SMEM, VMEM, VMEM, VMEM],
+        [SMEM] + [VMEM] * 5,
         place,
         hamiltonian,
         factor_rows,
         got,
+        r_first,
+        r_second,
         cost_estimate=cost,
     )
 

time: 92.8 us -> 105 us (1.13)
  starting transfers between devices: 12.7 us -> 36 us
  blocking collectives: 60.1 us -> 38.8 us
  waiting for transfers between devices: 8.88 us -> 17.9 us
    all_to_all x2 -> x1, blocking collectives: 60.1 us -> 38.8 us  [exchange(): return lax.all_to_all(payload, axis, 0, 0)]
    all_to_all x1 -> x2, starting transfers between devices: 10.4 us -> 27.7 us  [exchange(): return lax.all_to_all(payload, axis, 0, 0)]
    ppermute x1 -> x2, waiting for transfers between devices: 2.61 us -> 15.6 us  [per_device(): lax.ppermute(factor_rows, ('row', 'col'), pairs)]
    ppermute x1 -> x2, starting transfers between devices: 2.31 us -> 8.24 us  [per_device(): lax.ppermute(factor_rows, ('row', 'col'), pairs)]
    all_to_all x1 -> x2, waiting for transfers between devices: 6.27 us -> 2.24 us  [exchange(): return lax.all_to_all(payload, axis, 0, 0)]
    unnamed x4 -> x8, local copies, waits for them, and re-layouts: 0.01 us -> 2.2 us
    slice x2 -> x0, local copies, waits for them, and re-layouts: 1.86 us -> none  [the longest x1 1.02 us: per_device(): hamiltonian[:, :WIDE]]
  transfers between devices with their start and end apart: 2 -> 4, of which waited for: 2 -> 3; matrix products, arithmetic and copies ran while one was open for 0% -> 0% of each run, Pallas kernels for 0% -> 0%
where the time goes in v4:
time: 105 us
  blocking collectives  38.8 us (37%)
  starting transfers between devices  36 us (34%)
  waiting for transfers between devices  17.9 us (17%)
  Pallas kernels  9.63 us (9%)
  local copies, waits for them, and re-layouts  2.21 us (2%)
    all_to_all x1, blocking collectives, exchange(): return lax.all_to_all(payload, axis, 0, 0)  38.8 us
    all_to_all x2, starting transfers between devices, exchange(): return lax.all_to_all(payload, axis, 0, 0)  27.7 us
    ppermute x2, waiting for transfers between devices, per_device(): lax.ppermute(factor_rows, ('row', 'col'), pairs)  15.6 us
    pallas_call x4, Pallas kernels, call(): pl.pallas_call(function, out_shape=jax.ShapeDtypeStruct(shape, jnp.float3...  9.63 us
    ppermute x2, starting transfers between devices, per_device(): lax.ppermute(factor_rows, ('row', 'col'), pairs)  8.24 us
    all_to_all x2, waiting for transfers between devices, exchange(): return lax.all_to_all(payload, axis, 0, 0)  2.24 us
    unnamed x8, local copies, waits for them, and re-layouts  2.2 us
  transfers between devices with their start and end apart: 4, of which 3 were waited for; matrix products, arithmetic and copies ran while one was open for 0% of the time, Pallas kernels for 0%

profile of v4, /device:TPU:8, one launch (start us, length us, event | category | flops | bytes accessed | tf_op | source)
XLA Modules:
  0.0 104.6 jit_solution(655982582354747506)
XLA Ops:
  0.0 0.0 copy-start
  0.0 1.3 %copy-done = f32[768,384]{1,0:T(8,128)S(1)} copy-done((f32[768,384]{1,0:T(8,128)S(1)}, f32[768,384]{1,0:T(8,128)}, u32[]{:S(2)}) %copy-start) | copy-done | bytes 1179672
  1.3 0.0 copy-start.2
  1.3 0.9 copy-done.2
  2.2 0.0 copy-start.3
  2.2 0.8 shard_map.28
  3.0 10.2 %all-to-all-start = ((f32[32,2,8,128]{3,2,1,0:T(8,128)}), f32[32,2,8,128]{3,2,1,0:T(8,128)S(1)}, u32[]{:S(2)}, u32[]{:S(2)}) async-start(f32[32,2,8,128]{3,2,1,0:T(8,128)} %shard_map.28), calls=%async_computation | async-start | bytes 524288 | tf_op jit(solution)/shard_map/all_to_all | solution.py:152
  13.2 0.0 copy-done.3
  13.2 1.9 %collective-permute-start = (f32[128,384]{1,0:T(8,128)S(1)}, f32[128,384]{1,0:T(8,128)S(1)}, u32[]{:S(2)}, u32[]{:S(2)}) collective-permute-start(f32[128,384]{1,0:T(8,128)S(1)} %copy-done.3), channel_id=1, source_target_pairs={{0,0},{1,33},{2,66},{3,99},{4,132},{5,165},{6,198},{7,231},{8,256}... | collective-permute-start | bytes 589832 | tf_op jit(solution)/shard_map/ppermute | solution.py:168
  15.1 8.1 %collective-permute-done.ra_ref = f32[128,384]{1,0:T(8,128)S(1)} collective-permute-done((f32[128,384]{1,0:T(8,128)S(1)}, f32[128,384]{1,0:T(8,128)S(1)}, u32[]{:S(2)}, u32[]{:S(2)}) %collective-permute-start) | collective-permute-done | bytes 196640 | tf_op jit(solution)/shard_map/ppermute | solution.py:168
  23.3 2.2 %all-to-all-done = f32[32,2,8,128]{3,2,1,0:T(8,128)S(1)} async-done(((f32[32,2,8,128]{3,2,1,0:T(8,128)}), f32[32,2,8,128]{3,2,1,0:T(8,128)S(1)}, u32[]{:S(2)}, u32[]{:S(2)}) %all-to-all-start) | async-done | bytes 262176 | tf_op jit(solution)/shard_map/all_to_all | solution.py:152
  25.5 0.8 shard_map.29
  26.3 17.6 %all-to-all-start.1 = ((f32[16,4,8,128]{3,2,1,0:T(8,128)}), f32[16,4,8,128]{3,2,1,0:T(8,128)S(1)}, u32[]{:S(2)}, u32[]{:S(2)}) async-start(f32[16,4,8,128]{3,2,1,0:T(8,128)} %shard_map.29), calls=%async_computation.1 | async-start | bytes 524288 | tf_op jit(solution)/shard_map/all_to_all | solution.py:152
  43.9 6.3 %collective-permute-start.1 = (f32[128,384]{1,0:T(8,128)S(1)}, f32[128,384]{1,0:T(8,128)S(1)}, u32[]{:S(2)}, u32[]{:S(2)}) collective-permute-start(f32[128,384]{1,0:T(8,128)S(1)} %copy-done.3), channel_id=1, source_target_pairs={{0,10},{1,43},{2,76},{3,109},{4,142},{5,175},{6,200},{7,233},{8,26... | collective-permute-start | bytes 589832 | tf_op jit(solution)/shard_map/ppermute | solution.py:168
  50.2 0.1 pad_add_fusion.place
  50.3 0.0 copy-start.1
  50.3 7.5 %collective-permute-done.1.rb_ref = f32[128,384]{1,0:T(8,128)S(1)} collective-permute-done((f32[128,384]{1,0:T(8,128)S(1)}, f32[128,384]{1,0:T(8,128)S(1)}, u32[]{:S(2)}, u32[]{:S(2)}) %collective-permute-start.1) | collective-permute-done | bytes 196640 | tf_op jit(solution)/shard_map/ppermute | solution.py:168
  57.8 0.0 all-to-all-done.1.all_ref
  57.8 0.6 shard_map.30
  58.4 38.8 %all_to_all.15.got_ref = f32[32,6,8,128]{3,2,1,0:T(8,128)S(1)} all-to-all(f32[32,6,8,128]{3,2,1,0:T(8,128)S(1)} %shard_map.30), channel_id=1, replica_groups=mesh['row'=16,'col'=32] {'col'}, dimensions={0} | all-to-all | bytes 1572864 | tf_op jit(solution)/shard_map/all_to_all | solution.py:152
  97.2 0.0 copy-done.1
  97.2 7.4 %shard_map.31 = f32[768,384]{1,0:T(8,128)} custom-call(s32[2]{0:T(128)S(1)} %pad_add_fusion.place, f32[768,384]{1,0:T(8,128)S(1)} %copy-done.1, f32[128,384]{1,0:T(8,128)S(1)} %copy-done.3, f32[32,6,8,128]{3,2,1,0:T(8,128)S(1)} %all_to_all.15.got_ref, f32[128,384]{1,0:T(8,128)S(1)} %collective-permute-done.ra_ref, f32[128,384]{1,0:T(8,128)S(1)} %collective-permute-done.1.rb_ref), custom_call_target="tpu_custom_call" | custom-call | flops 1000000000 | bytes 5000000 | tf_op jit(solution)/shard_map/pallas_call | solution.py:141
  (1 shorter events, 0.0 us)
Async XLA Ops:
  0.0 1.3 %copy-start = (f32[768,384]{1,0:T(8,128)S(1)}, f32[768,384]{1,0:T(8,128)}, u32[]{:S(2)}) copy-start(f32[768,384]{1,0:T(8,128)} %h_ref.3) | copy-start | bytes 3538948
  1.3 0.9 copy-start.2
  2.2 11.0 %copy-start.3 = (f32[128,384]{1,0:T(8,128)S(1)}, f32[128,384]{1,0:T(8,128)}, u32[]{:S(2)}) copy-start(f32[128,384]{1,0:T(8,128)} %rj_ref.1) | copy-start | bytes 589828
  3.0 22.5 %all-to-all-start = ((f32[32,2,8,128]{3,2,1,0:T(8,128)}), f32[32,2,8,128]{3,2,1,0:T(8,128)S(1)}, u32[]{:S(2)}, u32[]{:S(2)}) async-start(f32[32,2,8,128]{3,2,1,0:T(8,128)} %shard_map.28), calls=%async_computation | async-start | bytes 524288 | tf_op jit(solution)/shard_map/all_to_all | solution.py:152
  13.2 10.0 %collective-permute-start = (f32[128,384]{1,0:T(8,128)S(1)}, f32[128,384]{1,0:T(8,128)S(1)}, u32[]{:S(2)}, u32[]{:S(2)}) collective-permute-start(f32[128,384]{1,0:T(8,128)S(1)} %copy-done.3), channel_id=1, source_target_pairs={{0,0},{1,33},{2,66},{3,99},{4,132},{5,165},{6,198},{7,231},{8,256}... | collective-permute-start | bytes 589832 | tf_op jit(solution)/shard_map/ppermute | solution.py:168
  26.3 31.5 %all-to-all-start.1 = ((f32[16,4,8,128]{3,2,1,0:T(8,128)}), f32[16,4,8,128]{3,2,1,0:T(8,128)S(1)}, u32[]{:S(2)}, u32[]{:S(2)}) async-start(f32[16,4,8,128]{3,2,1,0:T(8,128)} %shard_map.29), calls=%async_computation.1 | async-start | bytes 524288 | tf_op jit(solution)/shard_map/all_to_all | solution.py:152
  43.9 13.9 %collective-permute-start.1 = (f32[128,384]{1,0:T(8,128)S(1)}, f32[128,384]{1,0:T(8,128)S(1)}, u32[]{:S(2)}, u32[]{:S(2)}) collective-permute-start(f32[128,384]{1,0:T(8,128)S(1)} %copy-done.3), channel_id=1, source_target_pairs={{0,10},{1,43},{2,76},{3,109},{4,142},{5,175},{6,200},{7,233},{8,26... | collective-permute-start | bytes 589832 | tf_op jit(solution)/shard_map/ppermute | solution.py:168
  50.3 46.9 %copy-start.1 = (f32[768,384]{1,0:T(8,128)S(1)}, f32[768,384]{1,0:T(8,128)}, u32[]{:S(2)}) copy-start(f32[768,384]{1,0:T(8,128)} %h_ref.3) | copy-start | bytes 3538948

commit v5 on v3

v5 whole, which is shorter than its diff:
```python
import jax
import jax.numpy as jnp
from jax import lax
from jax.experimental import pallas as pl
from jax.experimental.pallas import tpu as pltpu
from jax.sharding import PartitionSpec as P

BLOCK = 64
WIDE = 2 * BLOCK
EXACT = lax.Precision.HIGHEST


def dot(left, right):
    return jnp.dot(left, right, precision=EXACT, preferred_element_type=jnp.float32)


def inner(left, right):
    return lax.dot_general(
        left, right, (((0,), (0,)), ((), ())), precision=EXACT, preferred_element_type=jnp.float32
    )


def wide_inverse(factor):
    row = lax.broadcasted_iota(jnp.int32, (WIDE, WIDE), 0)
    col = lax.broadcasted_iota(jnp.int32, (WIDE, WIDE), 1)
    on_diag = jnp.where(row == col, factor, 0.0)
    diag_col = jnp.sum(on_diag, axis=1, keepdims=True)
    diag_row = jnp.sum(on_diag, axis=0, keepdims=True)
    same = (row < BLOCK) == (col < BLOCK)
    power = jnp.where((row < col) & same, -factor / diag_col, 0.0)
    total = jnp.where(row == col, 1.0, power)
    power = dot(power, power)
    for _ in range(4):
        both = dot(jnp.concatenate([power, total], axis=0), power)
        power, total = both[:WIDE], total + both[WIDE:]
    total = (total + dot(total, power)) / diag_row
    couple = jnp.where((row < BLOCK) & (col >= BLOCK), factor, 0.0)
    return total - dot(total, dot(couple, total))


def beside(*parts):
    return jnp.concatenate(parts, axis=1)


def double_top(h_ref, out_ref, sems):
    copies = [
        pltpu.make_async_copy(
            h_ref.at[pl.ds(0, BLOCK)], out_ref.at[pl.ds(half * BLOCK, BLOCK)], sems.at[half]
        )
        for half in range(2)
    ]
    for copy in copies:
        copy.start()
    for copy in copies:
        copy.wait()


def pack_slab(place, slabs_ref, share_ref, slab_ref, out_ref):
    first = place[0] < slabs_ref.shape[0] // 2
    h_slab = jnp.where(first, slabs_ref[0], slabs_ref[1])
    packed = beside(h_slab, share_ref[...], slab_ref[:, :WIDE])
    for col in range(out_ref.shape[0]):
        out_ref[col] = packed


def pack_rows(place, slabs_ref, all_ref, out_ref):
    grid_rows, width = slabs_ref.shape[0], slabs_ref.shape[2]
    first = place[0] < grid_rows // 2
    own = jnp.where(first, slabs_ref[0], slabs_ref[1])
    left, right = all_ref[0], all_ref[1]
    tail = beside(
        own,
        left[:, :BLOCK],
        right[:, :BLOCK],
        left[:, 2 * width : 2 * width + BLOCK],
        right[:, 2 * width : 2 * width + BLOCK],
    )
    for row in range(grid_rows):
        out_ref[row, :, :width] = all_ref[row, :, :width]
        out_ref[row, :, width : 2 * width] = all_ref[row + grid_rows, :, :width]
        out_ref[row, :, 2 * width :] = tail


def body(place, h_ref, rj_ref, got_ref, all_ref, out_ref):
    grid_row, grid_col = place[0], place[1]
    width = rj_ref.shape[1]
    inverse = wide_inverse(got_ref[:, 3 * width + WIDE :])
    result = dot(inner(inverse, got_ref[:, 3 * width : 3 * width + WIDE]), inverse)
    weights = beside(inverse.T, -0.5 * result)
    r_own = rj_ref[...]
    z_own = dot(weights, jnp.concatenate([got_ref[:, 2 * width : 3 * width], r_own]))
    right = jnp.concatenate([z_own, r_own])
    lane = lax.broadcasted_iota(jnp.int32, (BLOCK, width), 1)
    inside = (lane >= BLOCK) | (grid_col >= 2)
    holders = all_ref.shape[0] // 2
    for section in range(2):
        r_rows = all_ref[section * holders : (section + 1) * holders, :, width : 2 * width]
        r_rows = r_rows.reshape(WIDE, width)
        h_rows = got_ref[:, section * width : (section + 1) * width]
        z_rows = dot(weights, jnp.concatenate([h_rows, r_rows]))
        change = inner(jnp.concatenate([r_rows, z_rows]), right)
        for m in range(width // BLOCK):
            rows = slice((2 * m + section) * BLOCK, (2 * m + section + 1) * BLOCK)
            part = change[m * BLOCK : (m + 1) * BLOCK]
            out_ref[rows, :] = h_ref[rows, :] - jnp.where(inside, part, 0.0)

    @pl.when(grid_row < 2)
    def _():
        pending = z_own - 0.5 * dot(result, r_own)
        old = h_ref[:BLOCK, :]
        first = grid_row == 0
        rest = jnp.where(first, pending[:BLOCK], pending[BLOCK:])
        lead = jnp.where(first, result[:BLOCK], result[BLOCK:])
        spread = beside(*[lead] * (width // WIDE))
        turned = beside(*[lead[:, BLOCK:], lead[:, :BLOCK]] * (width // WIDE))
        at_zero = jnp.where(first, spread, old)
        head = jnp.where(grid_col == 0, at_zero, turned)
        out_ref[:BLOCK, :] = jnp.where(inside, rest, head)


VMEM = pl.BlockSpec(memory_space=pltpu.VMEM)
SMEM = pl.BlockSpec(memory_space=pltpu.SMEM)


def call(function, shape, specs, *operands, **more):
    return pl.pallas_call(
        function,
        out_shape=jax.ShapeDtypeStruct(shape, jnp.float32),
        in_specs=specs,
        out_specs=VMEM,
        compiler_params=pltpu.CompilerParams(vmem_limit_bytes=40 * 1024 * 1024),
        **more,
    )(*operands)


def exchange(payload, axis):
    return lax.all_to_all(payload, axis, 0, 0)


def per_device(hamiltonian, factor_rows):
    grid_rows, grid_cols = lax.axis_size("row"), lax.axis_size("col")
    row_index, col_index = lax.axis_index("row"), lax.axis_index("col")
    place = jnp.stack([row_index, col_index])
    width = hamiltonian.shape[1]
    slab = WIDE // grid_rows

    pairs = [
        (r * grid_cols + c, (c % grid_rows) * grid_cols + grid_rows * (c // grid_rows) + r)
        for r in range(grid_rows)
        for c in range(grid_cols)
    ]
    r_slab = lax.dynamic_slice_in_dim(factor_rows, row_index * slab, slab, 0)
    r_share = lax.ppermute(r_slab, ("row", "col"), pairs)

    top = call(
        double_top,
        (WIDE, width),
        [pl.BlockSpec(memory_space=pl.ANY)],
        hamiltonian,
        scratch_shapes=[pltpu.SemaphoreType.DMA((2,))],
    )
    slabs = exchange(top.reshape(grid_rows, slab, width), "row")
    shape = (grid_cols, slab, 2 * width + WIDE)
    everything = call(
        pack_slab, shape, [SMEM, VMEM, VMEM, VMEM], place, slabs, r_share, r_slab
    )
    everything = exchange(everything, "col")
    shape = (grid_rows, slab, 3 * width + 2 * WIDE)
    got = call(pack_rows, shape, [SMEM, VMEM, VMEM], place, slabs, everything)
    got = exchange(got, "row").reshape(WIDE, -1)
    cost = pl.CostEstimate(flops=10**9, bytes_accessed=5 * 10**6, transcendentals=0)
    return call(
        body,
        hamiltonian.shape,
        [SMEM] + [VMEM] * 4,
        place,
        hamiltonian,
        factor_rows,
        got,
        everything,
        cost_estimate=cost,
    )


def solution(mesh):
    placed = (P("row", "col"), P(None, "col"))
    return jax.shard_map(
        per_device, mesh=mesh, in_specs=placed, out_specs=P("row", "col"), check_vma=False
    )
```

time: 92.8 us -> 99 us (1.067)
  the two profiles are of different devices: /device:TPU:8 before, /device:TPU:1 now
where the time goes in v5:
time: 99 us; the launch traced here: 98.6 us
  blocking collectives  66.1 us (67%)
  starting transfers between devices  15 us (15%)
  Pallas kernels  9.08 us (9%)
  waiting for transfers between devices  7.01 us (7%)
  local copies, waits for them, and re-layouts  1.29 us (1%)
    all_to_all x2, blocking collectives, exchange(): return lax.all_to_all(payload, axis, 0, 0)  66.1 us
    all_to_all x1, starting transfers between devices, exchange(): return lax.all_to_all(payload, axis, 0, 0)  11.8 us
    pallas_call x4, Pallas kernels, call(): pl.pallas_call(function, out_shape=jax.ShapeDtypeStruct(shape, jnp.float3...  9.08 us
    all_to_all x1, waiting for transfers between devices, exchange(): return lax.all_to_all(payload, axis, 0, 0)  4.99 us
    ppermute x1, starting transfers between devices, per_device(): r_share = lax.ppermute(r_slab, ('row', 'col'), pairs)  3.2 us
    ppermute x1, waiting for transfers between devices, per_device(): r_share = lax.ppermute(r_slab, ('row', 'col'), pairs)  2.02 us
  transfers between devices with their start and end apart: 2, of which 2 were waited for; matrix products, arithmetic and copies ran while one was open for 0% of the time, Pallas kernels for 0%

profile of v5, /device:TPU:1, one launch (start us, length us, event | category | flops | bytes accessed | tf_op | source)
XLA Modules:
  0.0 98.6 jit_solution(1230456477492849239)
XLA Ops:
  0.0 0.0 copy-start
  0.0 1.3 %copy-done = f32[768,384]{1,0:T(8,128)S(1)} copy-done((f32[768,384]{1,0:T(8,128)S(1)}, f32[768,384]{1,0:T(8,128)}, u32[]{:S(2)}) %copy-start) | copy-done | bytes 1179672
  1.3 0.0 copy-start.2
  1.3 0.9 shard_map.28
  2.2 11.8 %all-to-all-start = ((f32[16,8,384]{2,1,0:T(8,128)}), f32[16,8,384]{2,1,0:T(8,128)S(1)}, u32[]{:S(2)}, u32[]{:S(2)}) async-start(f32[16,8,384]{2,1,0:T(8,128)} %bitcast.2), calls=%async_computation | async-start | bytes 393216 | tf_op jit(solution)/shard_map/all_to_all | solution.py:137
  14.1 0.0 copy-done.2
  14.1 3.2 %collective-permute-start = (f32[8,384]{1,0:T(8,128)S(1)}, f32[8,384]{1,0:T(8,128)S(1)}, u32[]{:S(2)}, u32[]{:S(2)}) collective-permute-start(f32[8,384]{1,0:T(8,128)S(1)} %constant_dynamic-slice_fusion.slab_ref), channel_id=1, source_target_pairs={{0,0},{1,32},{2,64},{3,96},{4,128},{5,160},{6,192},{7,224},{8,256}... | collective-permute-start | bytes 36872 | tf_op jit(solution)/shard_map/ppermute | solution.py:153
  17.3 0.1 pad_add_fusion.place
  17.4 2.0 %collective-permute-done.share_ref = f32[8,384]{1,0:T(8,128)S(1)} collective-permute-done((f32[8,384]{1,0:T(8,128)S(1)}, f32[8,384]{1,0:T(8,128)S(1)}, u32[]{:S(2)}, u32[]{:S(2)}) %collective-permute-start) | collective-permute-done | bytes 12320 | tf_op jit(solution)/shard_map/ppermute | solution.py:153
  19.4 5.0 %all-to-all-done.slabs_ref = f32[16,8,384]{2,1,0:T(8,128)S(1)} async-done(((f32[16,8,384]{2,1,0:T(8,128)}), f32[16,8,384]{2,1,0:T(8,128)S(1)}, u32[]{:S(2)}, u32[]{:S(2)}) %all-to-all-start) | async-done | bytes 196640 | tf_op jit(solution)/shard_map/all_to_all | solution.py:137
  24.4 0.6 shard_map.29
  25.0 33.1 %all_to_all.15.all_ref = f32[32,8,896]{2,1,0:T(8,128)S(1)} all-to-all(f32[32,8,896]{2,1,0:T(8,128)S(1)} %shard_map.29), channel_id=1, replica_groups=mesh['row'=16,'col'=32] {'col'}, dimensions={0} | all-to-all | bytes 1835008 | tf_op jit(solution)/shard_map/all_to_all | solution.py:137
  58.0 0.6 shard_map.30
  58.7 0.0 copy-start.1
  58.7 33.0 %all_to_all.16 = f32[16,8,1408]{2,1,0:T(8,128)S(1)} all-to-all(f32[16,8,1408]{2,1,0:T(8,128)S(1)} %shard_map.30), channel_id=1, replica_groups=mesh['row'=16,'col'=32] {'row'}, dimensions={0} | all-to-all | bytes 1441792 | tf_op jit(solution)/shard_map/all_to_all | solution.py:137
  91.7 0.0 copy-done.1
  91.7 6.9 %shard_map.31 = f32[768,384]{1,0:T(8,128)} custom-call(s32[2]{0:T(128)S(1)} %pad_add_fusion.place, f32[768,384]{1,0:T(8,128)S(1)} %copy-done.1, f32[128,384]{1,0:T(8,128)S(1)} %copy-done.2, f32[128,1408]{1,0:T(8,128)S(1)} %bitcast.4, f32[32,8,896]{2,1,0:T(8,128)S(1)} %all_to_all.15.all_ref), custom_call_target="tpu_custom_call" | custom-call | flops 1000000000 | bytes 5000000 | tf_op jit(solution)/shard_map/pallas_call | solution.py:126
  (1 shorter events, 0.0 us)
Async XLA Ops:
  0.0 1.3 %copy-start = (f32[768,384]{1,0:T(8,128)S(1)}, f32[768,384]{1,0:T(8,128)}, u32[]{:S(2)}) copy-start(f32[768,384]{1,0:T(8,128)} %h_ref.3) | copy-start | bytes 3538948
  1.3 12.8 %copy-start.2 = (f32[128,384]{1,0:T(8,128)S(1)}, f32[128,384]{1,0:T(8,128)}, u32[]{:S(2)}) copy-start(f32[128,384]{1,0:T(8,128)} %rj_ref.1) | copy-start | bytes 589828
  2.2 22.2 %all-to-all-start = ((f32[16,8,384]{2,1,0:T(8,128)}), f32[16,8,384]{2,1,0:T(8,128)S(1)}, u32[]{:S(2)}, u32[]{:S(2)}) async-start(f32[16,8,384]{2,1,0:T(8,128)} %bitcast.2), calls=%async_computation | async-start | bytes 393216 | tf_op jit(solution)/shard_map/all_to_all | solution.py:137
  14.1 5.3 %collective-permute-start = (f32[8,384]{1,0:T(8,128)S(1)}, f32[8,384]{1,0:T(8,128)S(1)}, u32[]{:S(2)}, u32[]{:S(2)}) collective-permute-start(f32[8,384]{1,0:T(8,128)S(1)} %constant_dynamic-slice_fusion.slab_ref), channel_id=1, source_target_pairs={{0,0},{1,32},{2,64},{3,96},{4,128},{5,160},{6,192},{7,224},{8,256}... | collective-permute-start | bytes 36872 | tf_op jit(solution)/shard_map/ppermute | solution.py:153
  58.7 33.0 %copy-start.1 = (f32[768,384]{1,0:T(8,128)S(1)}, f32[768,384]{1,0:T(8,128)}, u32[]{:S(2)}) copy-start(f32[768,384]{1,0:T(8,128)} %h_ref.3) | copy-start | bytes 3538948

commit v6 on v3

--- a/solution.py
+++ b/solution.py
@@ -66,7 +66,7 @@
             out_ref[row, 2 * slot + 1] = high
 
 
-def pack_gather(place, all_ref, r_ref, out_ref):
+def pack_gather(place, all_ref, out_ref):
     grid_row, grid_col = place[0], place[1]
     grid_rows, grid_cols = all_ref.shape[0], out_ref.shape[0]
     own = all_ref[grid_row]
@@ -81,13 +81,13 @@
         out_ref[col, 3] = all_ref[col % grid_rows, lead]
         out_ref[col, 4] = all_ref[col % grid_rows, 2]
         out_ref[col, 5] = corner
-        for k in range(3):
-            out_ref[col, 6 + k] = r_ref[:, k * WIDE : (k + 1) * WIDE]
-
-
-def body(place, h_ref, rj_ref, got_ref, out_ref):
+
+
+def body(place, h_ref, rj_ref, got_ref, r_all_ref, out_ref, r_ref, sem):
     grid_row, grid_col = place[0], place[1]
     width = rj_ref.shape[1]
+    fetch = pltpu.make_async_copy(r_all_ref.at[:, pl.ds(0, 8)], r_ref, sem)
+    fetch.start()
     corner = got_ref[:, 5].reshape(2, WIDE, WIDE)
     inverse = wide_inverse(corner[1])
     result = dot(inner(inverse, corner[0]), inverse)
@@ -106,13 +106,9 @@
     across = jnp.concatenate([-0.5 * result.T, inverse], axis=0)
     lane = lax.broadcasted_iota(jnp.int32, (BLOCK, width), 1)
     inside = (lane >= BLOCK) | (grid_col >= 2)
+    fetch.wait()
     for section in range(2):
-        r_piece = jnp.concatenate(
-            [
-                got_ref[16 * section : 16 * section + 16, 6 + k].reshape(WIDE, WIDE).T
-                for k in range(width // WIDE)
-            ]
-        )
+        r_piece = r_ref[16 * section : 16 * section + 16].reshape(WIDE, width).T
         h_piece = []
         for m in range(width // BLOCK):
             group, k = owner_of(2 * m + section)
@@ -171,6 +167,8 @@
     r_slab = lax.dynamic_slice_in_dim(factor_rows, row_index * slab, slab, 0)
     r_share = lax.ppermute(r_slab, ("row", "col"), pairs)
 
+    r_all = lax.all_gather(jnp.concatenate([r_share] * 4), "col")
+
     halves = call(
         pack_columns,
         (grid_cols, 2, 8, WIDE),
@@ -178,21 +176,25 @@
         hamiltonian[:, :WIDE],
         factor_rows[:, :WIDE],
     )
+    halves, r_share = lax.optimization_barrier((halves, r_share))
     halves = exchange(halves, "col")
     share = call(pack_share, (grid_rows, 4, 8, WIDE), [VMEM], halves[:2])
     shares = exchange(share, "row")
-    offer = call(pack_gather, (grid_cols, 9, 8, WIDE), [SMEM, VMEM, VMEM], place, shares, r_share)
+    offer = call(pack_gather, (grid_cols, 6, 8, WIDE), [SMEM, VMEM], place, shares)
     got = exchange(offer, "col")
+    got, r_all = lax.optimization_barrier((got, r_all))
     cost = pl.CostEstimate(flops=10**9, bytes_accessed=5 * 10**6, transcendentals=0)
     return call(
         body,
         hamiltonian.shape,
-        [SMEM, VMEM, VMEM, VMEM],
+        [SMEM, VMEM, VMEM, VMEM, pl.BlockSpec(memory_space=pl.ANY)],
         place,
         hamiltonian,
         factor_rows,
         got,
+        r_all,
         cost_estimate=cost,
+        scratch_shapes=[pltpu.VMEM((grid_cols, 8, hamiltonian.shape[1]), jnp.float32), pltpu.SemaphoreType.DMA],
     )
 
 

time: 92.8 us -> 126 us (1.36)
  the two profiles are of different devices: /device:TPU:8 before, /device:TPU:1 now
where the time goes in v6:
time: 126 us; the launch traced here: 124 us
  blocking collectives  52.8 us (42%)
  waiting for transfers between devices  25 us (20%)
  starting transfers between devices  19.1 us (15%)
  between operations  13.4 us (11%)
  Pallas kernels  8.93 us (7%)
  local copies, waits for them, and re-layouts  3.99 us (3%)
    all_to_all x2, blocking collectives, exchange(): return lax.all_to_all(payload, axis, 0, 0)  52.8 us
    all_to_all x1, starting transfers between devices, exchange(): return lax.all_to_all(payload, axis, 0, 0)  14.5 us
    all_gather x1, waiting for transfers between devices, per_device(): r_all = lax.all_gather(jnp.concatenate([r_share] * 4), 'col')  12 us
    all_to_all x1, waiting for transfers between devices, exchange(): return lax.all_to_all(payload, axis, 0, 0)  11.6 us
    pallas_call x4, Pallas kernels, call(): pl.pallas_call(function, out_shape=jax.ShapeDtypeStruct(shape, jnp.float3...  8.93 us
    ppermute x1, starting transfers between devices, per_device(): r_share = lax.ppermute(r_slab, ('row', 'col'), pairs)  4.58 us
  transfers between devices with their start and end apart: 3, of which 3 were waited for; matrix products, arithmetic and copies ran while one was open for 2% of the time, Pallas kernels for 1%

profile of v6, /device:TPU:1, one launch (start us, length us, event | category | flops | bytes accessed | tf_op | source)
XLA Modules:
  0.0 124.0 jit_solution(13549426844707180240)
XLA Ops:
  6.5 0.0 all-gather.3.cloned.1.call-start
  6.5 0.7 constant_dynamic-slice_fusion
  7.2 4.6 %collective-permute-start = (f32[8,384]{1,0:T(8,128)S(1)}, f32[8,384]{1,0:T(8,128)S(1)}, u32[]{:S(2)}, u32[]{:S(2)}) collective-permute-start(f32[8,384]{1,0:T(8,128)S(1)} %constant_dynamic-slice_fusion), channel_id=1, source_target_pairs={{0,0},{1,32},{2,64},{3,96},{4,128},{5,160},{6,192},{7,224},{8,256}... | collective-permute-start | bytes 36872 | tf_op jit(solution)/shard_map/ppermute | solution.py:168
  11.8 1.4 %collective-permute-done = f32[8,384]{1,0:T(8,128)S(1)} collective-permute-done((f32[8,384]{1,0:T(8,128)S(1)}, f32[8,384]{1,0:T(8,128)S(1)}, u32[]{:S(2)}, u32[]{:S(2)}) %collective-permute-start) | collective-permute-done | bytes 12320 | tf_op jit(solution)/shard_map/ppermute | solution.py:168
  13.2 0.6 pad_maximum_fusion
  13.8 0.0 all-gather.3.cloned.1.call-update
  13.8 0.8 slice.10.r_ref
  14.7 1.0 slice.9.h_ref
  15.7 0.1 shard_map.28
  15.8 26.2 %all_to_all.15 = f32[32,2,8,128]{3,2,1,0:T(8,128)S(1)} all-to-all(f32[32,2,8,128]{3,2,1,0:T(8,128)S(1)} %shard_map.28), channel_id=1, replica_groups=mesh['row'=16,'col'=32] {'col'}, dimensions={0} | all-to-all | bytes 524288 | tf_op jit(solution)/shard_map/all_to_all | solution.py:153
  42.1 0.8 shard_map.29
  42.9 14.5 %all-to-all-start.1 = ((f32[16,4,8,128]{3,2,1,0:T(8,128)}), f32[16,4,8,128]{3,2,1,0:T(8,128)S(1)}, u32[]{:S(2)}, u32[]{:S(2)}) async-start(f32[16,4,8,128]{3,2,1,0:T(8,128)} %shard_map.29), calls=%async_computation.1 | async-start | bytes 524288 | tf_op jit(solution)/shard_map/all_to_all | solution.py:153
  57.4 0.1 pad_add_fusion.place
  57.4 0.0 copy-start
  57.4 0.0 copy-start.2
  57.4 11.6 %all-to-all-done.1.all_ref = f32[16,4,8,128]{3,2,1,0:T(8,128)S(1)} async-done(((f32[16,4,8,128]{3,2,1,0:T(8,128)}), f32[16,4,8,128]{3,2,1,0:T(8,128)S(1)}, u32[]{:S(2)}, u32[]{:S(2)}) %all-to-all-start.1) | async-done | bytes 262176 | tf_op jit(solution)/shard_map/all_to_all | solution.py:153
  69.1 0.6 shard_map.30
  69.7 26.6 %all_to_all.16.got_ref = f32[32,6,8,128]{3,2,1,0:T(8,128)S(1)} all-to-all(f32[32,6,8,128]{3,2,1,0:T(8,128)S(1)} %shard_map.30), channel_id=1, replica_groups=mesh['row'=16,'col'=32] {'col'}, dimensions={0} | all-to-all | bytes 1572864 | tf_op jit(solution)/shard_map/all_to_all | solution.py:153
  96.3 12.0 %all-gather.3.cloned.1.call-done = f32[1024,384]{1,0:T(8,128)} async-done(((f32[32,384]{1,0:T(8,128)}), f32[1024,384]{1,0:T(8,128)}) %all-gather.3.cloned.1.call-update) | async-done | bytes 1572880 | tf_op jit(solution)/shard_map/all_gather | solution.py:170
  108.3 0.0 copy-done
  108.3 0.0 copy-done.2
  108.3 0.0 copy-start.1
  108.3 1.4 %copy-done.1 = f32[1024,384]{1,0:T(8,128)S(1)} copy-done((f32[1024,384]{1,0:T(8,128)S(1)}, f32[1024,384]{1,0:T(8,128)}, u32[]{:S(2)}) %copy-start.1) | copy-done | bytes 1572888
  109.7 7.4 %shard_map.31 = f32[768,384]{1,0:T(8,128)} custom-call(s32[2]{0:T(128)S(1)} %pad_add_fusion.place, f32[768,384]{1,0:T(8,128)S(1)} %copy-done, f32[128,384]{1,0:T(8,128)S(1)} %copy-done.2, f32[32,6,8,128]{3,2,1,0:T(8,128)S(1)} %all_to_all.16.got_ref, f32[32,32,384]{2,1,0:T(8,128)S(1)} %bitcast.3), custom_call_target="tpu_custom_call" | custom-call | flops 1000000000 | bytes 5000000 | tf_op jit(solution)/shard_map/pallas_call | solution.py:142
  (1 shorter events, 0.0 us)
Async XLA Ops:
  6.5 101.8 %all-gather.3.cloned.1.call-start = ((), (), s32[]{:S(2)}) async-start(), calls=%async_computation.3 | async-start | bytes 1622016 | tf_op jit(solution)/shard_map/all_gather | solution.py:170
  7.2 6.0 %collective-permute-start = (f32[8,384]{1,0:T(8,128)S(1)}, f32[8,384]{1,0:T(8,128)S(1)}, u32[]{:S(2)}, u32[]{:S(2)}) collective-permute-start(f32[8,384]{1,0:T(8,128)S(1)} %constant_dynamic-slice_fusion), channel_id=1, source_target_pairs={{0,0},{1,32},{2,64},{3,96},{4,128},{5,160},{6,192},{7,224},{8,256}... | collective-permute-start | bytes 36872 | tf_op jit(solution)/shard_map/ppermute | solution.py:168
  42.9 26.2 %all-to-all-start.1 = ((f32[16,4,8,128]{3,2,1,0:T(8,128)}), f32[16,4,8,128]{3,2,1,0:T(8,128)S(1)}, u32[]{:S(2)}, u32[]{:S(2)}) async-start(f32[16,4,8,128]{3,2,1,0:T(8,128)} %shard_map.29), calls=%async_computation.1 | async-start | bytes 524288 | tf_op jit(solution)/shard_map/all_to_all | solution.py:153
  57.4 50.9 %copy-start = (f32[768,384]{1,0:T(8,128)S(1)}, f32[768,384]{1,0:T(8,128)}, u32[]{:S(2)}) copy-start(f32[768,384]{1,0:T(8,128)} %h_ref.1) | copy-start | bytes 3538948
  57.4 50.9 %copy-start.2 = (f32[128,384]{1,0:T(8,128)S(1)}, f32[128,384]{1,0:T(8,128)}, u32[]{:S(2)}) copy-start(f32[128,384]{1,0:T(8,128)} %rj_ref.1) | copy-start | bytes 589828
  108.3 1.4 %copy-start.1 = (f32[1024,384]{1,0:T(8,128)S(1)}, f32[1024,384]{1,0:T(8,128)}, u32[]{:S(2)}) copy-start(f32[1024,384]{1,0:T(8,128)} %all-gather.3.cloned.1.call-done) | copy-start | bytes 4718596
Sparse Core Ops, SparseCore 0:
  14.0 94.2 all-gather.2

commit v7 on v3

--- a/solution.py
+++ b/solution.py
@@ -18,6 +18,18 @@
     return lax.dot_general(
         left, right, (((0,), (0,)), ((), ())), precision=EXACT, preferred_element_type=jnp.float32
     )
+
+
+def halves_of(matrix):
+    high = matrix.astype(jnp.bfloat16)
+    return high, (matrix - high.astype(jnp.float32)).astype(jnp.bfloat16)
+
+
+def split_dot(left, right):
+    (left_high, left_low), (right_high, right_low) = left, right
+    small = jnp.dot(left_high, right_low, preferred_element_type=jnp.float32)
+    small += jnp.dot(left_low, right_high, preferred_element_type=jnp.float32)
+    return small + jnp.dot(left_high, right_high, preferred_element_type=jnp.float32)
 
 
 def wide_inverse(factor):
@@ -29,10 +41,11 @@
     same = (row < BLOCK) == (col < BLOCK)
     power = jnp.where((row < col) & same, -factor / diag_col, 0.0)
     total = jnp.where(row == col, 1.0, power)
-    for _ in range(5):
-        power = dot(power, power)
-        total = total + dot(total, power)
-    total = total / diag_row
+    power = dot(power, power)
+    for _ in range(4):
+        both = dot(jnp.concatenate([power, total], axis=0), power)
+        power, total = both[:WIDE], total + both[WIDE:]
+    total = (total + dot(total, power)) / diag_row
     couple = jnp.where((row < BLOCK) & (col >= BLOCK), factor, 0.0)
     return total - dot(total, dot(couple, total))
 
@@ -46,7 +59,16 @@
     return (block + k) % 4, k
 
 
-def pack_columns(h_ref, r_ref, out_ref):
+def pack_columns(h_hbm, r_hbm, out_ref, h_ref, r_ref, sems):
+    first_lanes = pl.ds(0, WIDE)
+    copies = [
+        pltpu.make_async_copy(h_hbm.at[:, first_lanes], h_ref, sems.at[0]),
+        pltpu.make_async_copy(r_hbm.at[:, first_lanes], r_ref, sems.at[1]),
+    ]
+    for copy in copies:
+        copy.start()
+    for copy in copies:
+        copy.wait()
     h_cols, r_cols = h_ref[:, :BLOCK], r_ref[:, :BLOCK]
     first = h_cols[: 4 * BLOCK]
     second = jnp.concatenate([h_cols[7 * BLOCK : 8 * BLOCK], h_cols[4 * BLOCK : 7 * BLOCK]])
@@ -85,15 +107,16 @@
             out_ref[col, 6 + k] = r_ref[:, k * WIDE : (k + 1) * WIDE]
 
 
-def body(place, h_ref, rj_ref, got_ref, out_ref):
+def body(place, h_ref, rj_ref, got_ref, out_hbm, out_ref, sems):
     grid_row, grid_col = place[0], place[1]
     width = rj_ref.shape[1]
+    blocks = width // BLOCK
     corner = got_ref[:, 5].reshape(2, WIDE, WIDE)
     inverse = wide_inverse(corner[1])
     result = dot(inner(inverse, corner[0]), inverse)
     own_section = grid_col // 16
     h_own = []
-    for m in range(width // BLOCK):
+    for m in range(blocks):
         (even, k), (odd, _) = owner_of(2 * m), owner_of(2 * m + 1)
         group = jnp.where(own_section == 0, even, odd)
         slot = 4 if k == 2 else 3
@@ -102,11 +125,12 @@
     r_own = rj_ref[...]
     weights = beside(inverse.T, -0.5 * result)
     z_own = dot(weights, jnp.concatenate([h_own, r_own], axis=0))
-    right = jnp.concatenate([z_own, r_own], axis=0)
+    right = halves_of(jnp.concatenate([z_own, r_own], axis=0))
     across = jnp.concatenate([-0.5 * result.T, inverse], axis=0)
     lane = lax.broadcasted_iota(jnp.int32, (BLOCK, width), 1)
     inside = (lane >= BLOCK) | (grid_col >= 2)
-    for section in range(2):
+    copies = []
+    for section in (1, 0):
         r_piece = jnp.concatenate(
             [
                 got_ref[16 * section : 16 * section + 16, 6 + k].reshape(WIDE, WIDE).T
@@ -114,41 +138,53 @@
             ]
         )
         h_piece = []
-        for m in range(width // BLOCK):
+        for m in range(blocks):
             group, k = owner_of(2 * m + section)
             h_piece.append(got_ref[8 * group : 8 * group + 8, k].reshape(BLOCK, WIDE))
         z_piece = dot(beside(r_piece, jnp.concatenate(h_piece)), across)
-        change = dot(beside(r_piece, z_piece), right)
-        for m in range(width // BLOCK):
+        change = split_dot(halves_of(beside(r_piece, z_piece)), right)
+        for m in range(blocks):
             rows = slice((2 * m + section) * BLOCK, (2 * m + section + 1) * BLOCK)
             part = change[m * BLOCK : (m + 1) * BLOCK]
             out_ref[rows, :] = h_ref[rows, :] - jnp.where(inside, part, 0.0)
 
-    @pl.when(grid_row < 2)
-    def _():
-        pending = z_own - 0.5 * dot(result, r_own)
-        old = h_ref[:BLOCK, :]
-        first = grid_row == 0
-        rest = jnp.where(first, pending[:BLOCK], pending[BLOCK:])
-        lead = jnp.where(first, result[:BLOCK], result[BLOCK:])
-        spread = jnp.concatenate([lead] * (width // WIDE), axis=1)
-        turned = jnp.concatenate([beside(lead[:, BLOCK:], lead[:, :BLOCK])] * (width // WIDE), axis=1)
-        at_zero = jnp.where(first, spread, old)
-        head = jnp.where(grid_col == 0, at_zero, turned)
-        out_ref[:BLOCK, :] = jnp.where(inside, rest, head)
+        if section == 0:
+
+            @pl.when(grid_row < 2)
+            def _():
+                pending = z_own - 0.5 * dot(result, r_own)
+                old = h_ref[:BLOCK, :]
+                first = grid_row == 0
+                rest = jnp.where(first, pending[:BLOCK], pending[BLOCK:])
+                lead = jnp.where(first, result[:BLOCK], result[BLOCK:])
+                spread = jnp.concatenate([lead] * (width // WIDE), axis=1)
+                turned = beside(lead[:, BLOCK:], lead[:, :BLOCK])
+                turned = jnp.concatenate([turned] * (width // WIDE), axis=1)
+                at_zero = jnp.where(first, spread, old)
+                head = jnp.where(grid_col == 0, at_zero, turned)
+                out_ref[:BLOCK, :] = jnp.where(inside, rest, head)
+
+        for m in range(blocks):
+            rows = pl.ds((2 * m + section) * BLOCK, BLOCK)
+            copy = pltpu.make_async_copy(out_ref.at[rows], out_hbm.at[rows], sems.at[2 * m + section])
+            copy.start()
+            copies.append(copy)
+    for copy in copies:
+        copy.wait()
 
 
 VMEM = pl.BlockSpec(memory_space=pltpu.VMEM)
 SMEM = pl.BlockSpec(memory_space=pltpu.SMEM)
-
-
-def call(function, shape, specs, *operands, **more):
+ANY = pl.BlockSpec(memory_space=pl.ANY)
+
+
+def call(function, shape, specs, *operands, vmem=40, out=VMEM, **more):
     return pl.pallas_call(
         function,
         out_shape=jax.ShapeDtypeStruct(shape, jnp.float32),
         in_specs=specs,
-        out_specs=VMEM,
-        compiler_params=pltpu.CompilerParams(vmem_limit_bytes=40 * 1024 * 1024),
+        out_specs=out,
+        compiler_params=pltpu.CompilerParams(vmem_limit_bytes=vmem * 1024 * 1024),
         **more,
     )(*operands)
 
@@ -174,11 +210,18 @@
     halves = call(
         pack_columns,
         (grid_cols, 2, 8, WIDE),
-        [VMEM, VMEM],
-        hamiltonian[:, :WIDE],
-        factor_rows[:, :WIDE],
+        [ANY, ANY],
+        hamiltonian,
+        factor_rows,
+        vmem=58,
+        scratch_shapes=[
+            pltpu.VMEM((hamiltonian.shape[0], WIDE), jnp.float32),
+            pltpu.VMEM((WIDE, WIDE), jnp.float32),
+            pltpu.SemaphoreType.DMA((2,)),
+        ],
     )
     halves = exchange(halves, "col")
+    halves, r_share = lax.optimization_barrier((halves, r_share))
     share = call(pack_share, (grid_rows, 4, 8, WIDE), [VMEM], halves[:2])
     shares = exchange(share, "row")
     offer = call(pack_gather, (grid_cols, 9, 8, WIDE), [SMEM, VMEM, VMEM], place, shares, r_share)
@@ -193,6 +236,11 @@
         factor_rows,
         got,
         cost_estimate=cost,
+        out=ANY,
+        scratch_shapes=[
+            pltpu.VMEM(hamiltonian.shape, jnp.float32),
+            pltpu.SemaphoreType.DMA((hamiltonian.shape[0] // BLOCK,)),
+        ],
     )
 
 

time: 92.8 us -> 99.3 us (1.070)
  the two profiles are of different devices: /device:TPU:8 before, /device:TPU:1 now
where the time goes in v7:
time: 99.3 us; the launch traced here: 99 us
  blocking collectives  42.1 us (42%)
  starting transfers between devices  29.8 us (30%)
  waiting for transfers between devices  17 us (17%)
  Pallas kernels  9.9 us (10%)
    all_to_all x1, blocking collectives, exchange(): return lax.all_to_all(payload, axis, 0, 0)  42.1 us
    all_to_all x2, starting transfers between devices, exchange(): return lax.all_to_all(payload, axis, 0, 0)  25.5 us
    all_to_all x2, waiting for transfers between devices, exchange(): return lax.all_to_all(payload, axis, 0, 0)  13 us
    pallas_call x4, Pallas kernels, call(): pl.pallas_call(function, out_shape=jax.ShapeDtypeStruct(shape, jnp.float3...  9.9 us
    ppermute x1, starting transfers between devices, per_device(): r_share = lax.ppermute(r_slab, ('row', 'col'), pairs)  4.26 us
    ppermute x1, waiting for transfers between devices, per_device(): r_share = lax.ppermute(r_slab, ('row', 'col'), pairs)  4.02 us
  transfers between devices with their start and end apart: 3, of which 3 were waited for; matrix products, arithmetic and copies ran while one was open for 0% of the time, Pallas kernels for 0%

profile of v7, /device:TPU:1, one launch (start us, length us, event | category | flops | bytes accessed | tf_op | source)
XLA Modules:
  0.0 99.0 jit_solution(15566006130310248902)
XLA Ops:
  0.0 0.0 copy-start.1
  0.0 1.9 %shard_map.28 = f32[32,2,8,128]{3,2,1,0:T(8,128)} custom-call(f32[768,384]{1,0:T(8,128)} %h_ref.1, f32[128,384]{1,0:T(8,128)} %rj_ref.1), custom_call_target="tpu_custom_call" | custom-call | tf_op jit(solution)/shard_map/pallas_call | solution.py:182
  1.9 10.5 %all-to-all-start = ((f32[32,2,8,128]{3,2,1,0:T(8,128)}), f32[32,2,8,128]{3,2,1,0:T(8,128)S(1)}, u32[]{:S(2)}, u32[]{:S(2)}) async-start(f32[32,2,8,128]{3,2,1,0:T(8,128)} %shard_map.28), calls=%async_computation | async-start | bytes 524288 | tf_op jit(solution)/shard_map/all_to_all | solution.py:193
  12.4 0.0 copy-done.1
  12.4 4.3 %collective-permute-start = (f32[8,384]{1,0:T(8,128)S(1)}, f32[8,384]{1,0:T(8,128)S(1)}, u32[]{:S(2)}, u32[]{:S(2)}) collective-permute-start(f32[8,384]{1,0:T(8,128)S(1)} %constant_dynamic-slice_fusion), channel_id=1, source_target_pairs={{0,0},{1,32},{2,64},{3,96},{4,128},{5,160},{6,192},{7,224},{8,256}... | collective-permute-start | bytes 36872 | tf_op jit(solution)/shard_map/ppermute | solution.py:208
  16.7 4.0 %collective-permute-done.r_ref = f32[8,384]{1,0:T(8,128)S(1)} collective-permute-done((f32[8,384]{1,0:T(8,128)S(1)}, f32[8,384]{1,0:T(8,128)S(1)}, u32[]{:S(2)}, u32[]{:S(2)}) %collective-permute-start) | collective-permute-done | bytes 12320 | tf_op jit(solution)/shard_map/ppermute | solution.py:208
  20.7 1.4 %all-to-all-done = f32[32,2,8,128]{3,2,1,0:T(8,128)S(1)} async-done(((f32[32,2,8,128]{3,2,1,0:T(8,128)}), f32[32,2,8,128]{3,2,1,0:T(8,128)S(1)}, u32[]{:S(2)}, u32[]{:S(2)}) %all-to-all-start) | async-done | bytes 262176 | tf_op jit(solution)/shard_map/all_to_all | solution.py:193
  22.1 0.8 shard_map.29
  22.9 15.0 %all-to-all-start.1 = ((f32[16,4,8,128]{3,2,1,0:T(8,128)}), f32[16,4,8,128]{3,2,1,0:T(8,128)S(1)}, u32[]{:S(2)}, u32[]{:S(2)}) async-start(f32[16,4,8,128]{3,2,1,0:T(8,128)} %shard_map.29), calls=%async_computation.1 | async-start | bytes 524288 | tf_op jit(solution)/shard_map/all_to_all | solution.py:193
  37.9 0.1 pad_add_fusion.place
  38.0 11.6 %all-to-all-done.1.all_ref = f32[16,4,8,128]{3,2,1,0:T(8,128)S(1)} async-done(((f32[16,4,8,128]{3,2,1,0:T(8,128)}), f32[16,4,8,128]{3,2,1,0:T(8,128)S(1)}, u32[]{:S(2)}, u32[]{:S(2)}) %all-to-all-start.1) | async-done | bytes 262176 | tf_op jit(solution)/shard_map/all_to_all | solution.py:193
  49.6 0.6 shard_map.30
  50.3 0.0 copy-start
  50.3 42.1 %all_to_all.15.got_ref = f32[32,9,8,128]{3,2,1,0:T(8,128)S(1)} all-to-all(f32[32,9,8,128]{3,2,1,0:T(8,128)S(1)} %shard_map.30), channel_id=1, replica_groups=mesh['row'=16,'col'=32] {'col'}, dimensions={0} | all-to-all | bytes 2359296 | tf_op jit(solution)/shard_map/all_to_all | solution.py:193
  92.3 0.0 copy-done
  92.3 6.6 %shard_map.31 = f32[768,384]{1,0:T(8,128)} custom-call(s32[2]{0:T(128)S(1)} %pad_add_fusion.place, f32[768,384]{1,0:T(8,128)S(1)} %copy-done, f32[128,384]{1,0:T(8,128)S(1)} %copy-done.1, f32[32,9,8,128]{3,2,1,0:T(8,128)S(1)} %all_to_all.15.got_ref), custom_call_target="tpu_custom_call" | custom-call | flops 1000000000 | bytes 5000000 | tf_op jit(solution)/shard_map/pallas_call | solution.py:182
  (2 shorter events, 0.0 us)
Async XLA Ops:
  0.0 12.4 %copy-start.1 = (f32[128,384]{1,0:T(8,128)S(1)}, f32[128,384]{1,0:T(8,128)}, u32[]{:S(2)}) copy-start(f32[128,384]{1,0:T(8,128)} %rj_ref.1) | copy-start | bytes 589828
  1.9 20.2 %all-to-all-start = ((f32[32,2,8,128]{3,2,1,0:T(8,128)}), f32[32,2,8,128]{3,2,1,0:T(8,128)S(1)}, u32[]{:S(2)}, u32[]{:S(2)}) async-start(f32[32,2,8,128]{3,2,1,0:T(8,128)} %shard_map.28), calls=%async_computation | async-start | bytes 524288 | tf_op jit(solution)/shard_map/all_to_all | solution.py:193
  12.4 8.3 %collective-permute-start = (f32[8,384]{1,0:T(8,128)S(1)}, f32[8,384]{1,0:T(8,128)S(1)}, u32[]{:S(2)}, u32[]{:S(2)}) collective-permute-start(f32[8,384]{1,0:T(8,128)S(1)} %constant_dynamic-slice_fusion), channel_id=1, source_target_pairs={{0,0},{1,32},{2,64},{3,96},{4,128},{5,160},{6,192},{7,224},{8,256}... | collective-permute-start | bytes 36872 | tf_op jit(solution)/shard_map/ppermute | solution.py:208
  22.9 26.7 %all-to-all-start.1 = ((f32[16,4,8,128]{3,2,1,0:T(8,128)}), f32[16,4,8,128]{3,2,1,0:T(8,128)S(1)}, u32[]{:S(2)}, u32[]{:S(2)}) async-start(f32[16,4,8,128]{3,2,1,0:T(8,128)} %shard_map.29), calls=%async_computation.1 | async-start | bytes 524288 | tf_op jit(solution)/shard_map/all_to_all | solution.py:193
  50.3 42.1 %copy-start = (f32[768,384]{1,0:T(8,128)S(1)}, f32[768,384]{1,0:T(8,128)}, u32[]{:S(2)}) copy-start(f32[768,384]{1,0:T(8,128)} %h_ref.1) | copy-start | bytes 3538948

commit v8 on v7

--- a/solution.py
+++ b/solution.py
@@ -221,7 +221,6 @@
         ],
     )
     halves = exchange(halves, "col")
-    halves, r_share = lax.optimization_barrier((halves, r_share))
     share = call(pack_share, (grid_rows, 4, 8, WIDE), [VMEM], halves[:2])
     shares = exchange(share, "row")
     offer = call(pack_gather, (grid_cols, 9, 8, WIDE), [SMEM, VMEM, VMEM], place, shares, r_share)

time: 99.3 us -> 92.4 us (0.931)
  the two profiles are of different devices: /device:TPU:1 before, /device:TPU:8 now
where the time goes in v8:
time: 92.4 us; the launch traced here: 92 us
  blocking collectives  60.3 us (65%)
  starting transfers between devices  12.7 us (14%)
  Pallas kernels  9.9 us (11%)
  waiting for transfers between devices  8.88 us (10%)
    all_to_all x2, blocking collectives, exchange(): return lax.all_to_all(payload, axis, 0, 0)  60.3 us
    all_to_all x1, starting transfers between devices, exchange(): return lax.all_to_all(payload, axis, 0, 0)  10.4 us
    pallas_call x4, Pallas kernels, call(): pl.pallas_call(function, out_shape=jax.ShapeDtypeStruct(shape, jnp.float3...  9.9 us
    all_to_all x1, waiting for transfers between devices, exchange(): return lax.all_to_all(payload, axis, 0, 0)  6.27 us
    ppermute x1, waiting for transfers between devices, per_device(): r_share = lax.ppermute(r_slab, ('row', 'col'), pairs)  2.61 us
    ppermute x1, starting transfers between devices, per_device(): r_share = lax.ppermute(r_slab, ('row', 'col'), pairs)  2.31 us
  transfers between devices with their start and end apart: 2, of which 2 were waited for; matrix products, arithmetic and copies ran while one was open for 0% of the time, Pallas kernels for 0%

profile of v8, /device:TPU:8, one launch (start us, length us, event | category | flops | bytes accessed | tf_op | source)
XLA Modules:
  0.0 92.0 jit_solution(674281454642596131)
XLA Ops:
  0.0 0.0 copy-start.1
  0.0 1.9 %shard_map.28 = f32[32,2,8,128]{3,2,1,0:T(8,128)} custom-call(f32[768,384]{1,0:T(8,128)} %h_ref.1, f32[128,384]{1,0:T(8,128)} %rj_ref.1), custom_call_target="tpu_custom_call" | custom-call | tf_op jit(solution)/shard_map/pallas_call | solution.py:182
  1.9 22.5 %all_to_all.15 = f32[32,2,8,128]{3,2,1,0:T(8,128)S(1)} all-to-all(f32[32,2,8,128]{3,2,1,0:T(8,128)} %shard_map.28), channel_id=1, replica_groups=mesh['row'=16,'col'=32] {'col'}, dimensions={0} | all-to-all | bytes 524288 | tf_op jit(solution)/shard_map/all_to_all | solution.py:193
  24.4 0.8 shard_map.29
  25.2 10.4 %all-to-all-start.1 = ((f32[16,4,8,128]{3,2,1,0:T(8,128)}), f32[16,4,8,128]{3,2,1,0:T(8,128)S(1)}, u32[]{:S(2)}, u32[]{:S(2)}) async-start(f32[16,4,8,128]{3,2,1,0:T(8,128)} %shard_map.29), calls=%async_computation.1 | async-start | bytes 524288 | tf_op jit(solution)/shard_map/all_to_all | solution.py:193
  35.6 0.0 copy-done.1
  35.6 2.3 %collective-permute-start = (f32[8,384]{1,0:T(8,128)S(1)}, f32[8,384]{1,0:T(8,128)S(1)}, u32[]{:S(2)}, u32[]{:S(2)}) collective-permute-start(f32[8,384]{1,0:T(8,128)S(1)} %constant_dynamic-slice_fusion), channel_id=1, source_target_pairs={{0,0},{1,32},{2,64},{3,96},{4,128},{5,160},{6,192},{7,224},{8,256}... | collective-permute-start | bytes 36872 | tf_op jit(solution)/shard_map/ppermute | solution.py:208
  37.9 0.1 pad_add_fusion.place
  38.0 2.6 %collective-permute-done.r_ref = f32[8,384]{1,0:T(8,128)S(1)} collective-permute-done((f32[8,384]{1,0:T(8,128)S(1)}, f32[8,384]{1,0:T(8,128)S(1)}, u32[]{:S(2)}, u32[]{:S(2)}) %collective-permute-start) | collective-permute-done | bytes 12320 | tf_op jit(solution)/shard_map/ppermute | solution.py:208
  40.6 6.3 %all-to-all-done.1.all_ref = f32[16,4,8,128]{3,2,1,0:T(8,128)S(1)} async-done(((f32[16,4,8,128]{3,2,1,0:T(8,128)}), f32[16,4,8,128]{3,2,1,0:T(8,128)S(1)}, u32[]{:S(2)}, u32[]{:S(2)}) %all-to-all-start.1) | async-done | bytes 262176 | tf_op jit(solution)/shard_map/all_to_all | solution.py:193
  46.9 0.6 shard_map.30
  47.5 0.0 copy-start
  47.5 37.9 %all_to_all.16.got_ref = f32[32,9,8,128]{3,2,1,0:T(8,128)S(1)} all-to-all(f32[32,9,8,128]{3,2,1,0:T(8,128)S(1)} %shard_map.30), channel_id=1, replica_groups=mesh['row'=16,'col'=32] {'col'}, dimensions={0} | all-to-all | bytes 2359296 | tf_op jit(solution)/shard_map/all_to_all | solution.py:193
  85.4 0.0 copy-done
  85.4 6.6 %shard_map.31 = f32[768,384]{1,0:T(8,128)} custom-call(s32[2]{0:T(128)S(1)} %pad_add_fusion.place, f32[768,384]{1,0:T(8,128)S(1)} %copy-done, f32[128,384]{1,0:T(8,128)S(1)} %copy-done.1, f32[32,9,8,128]{3,2,1,0:T(8,128)S(1)} %all_to_all.16.got_ref), custom_call_target="tpu_custom_call" | custom-call | flops 1000000000 | bytes 5000000 | tf_op jit(solution)/shard_map/pallas_call | solution.py:182
  (2 shorter events, 0.0 us)
Async XLA Ops:
  0.0 35.6 %copy-start.1 = (f32[128,384]{1,0:T(8,128)S(1)}, f32[128,384]{1,0:T(8,128)}, u32[]{:S(2)}) copy-start(f32[128,384]{1,0:T(8,128)} %rj_ref.1) | copy-start | bytes 589828
  25.2 21.7 %all-to-all-start.1 = ((f32[16,4,8,128]{3,2,1,0:T(8,128)}), f32[16,4,8,128]{3,2,1,0:T(8,128)S(1)}, u32[]{:S(2)}, u32[]{:S(2)}) async-start(f32[16,4,8,128]{3,2,1,0:T(8,128)} %shard_map.29), calls=%async_computation.1 | async-start | bytes 524288 | tf_op jit(solution)/shard_map/all_to_all | solution.py:193
  35.6 5.0 %collective-permute-start = (f32[8,384]{1,0:T(8,128)S(1)}, f32[8,384]{1,0:T(8,128)S(1)}, u32[]{:S(2)}, u32[]{:S(2)}) collective-permute-start(f32[8,384]{1,0:T(8,128)S(1)} %constant_dynamic-slice_fusion), channel_id=1, source_target_pairs={{0,0},{1,32},{2,64},{3,96},{4,128},{5,160},{6,192},{7,224},{8,256}... | collective-permute-start | bytes 36872 | tf_op jit(solution)/shard_map/ppermute | solution.py:208
  47.5 37.9 %copy-start = (f32[768,384]{1,0:T(8,128)S(1)}, f32[768,384]{1,0:T(8,128)}, u32[]{:S(2)}) copy-start(f32[768,384]{1,0:T(8,128)} %h_ref.1) | copy-start | bytes 3538948
